TPU v7x, 128 devices: a whole 4x4x4 slice. The times are simulated.
128 devices in a mesh: group: 2 (over x_hi), gx: 8 (over y, core), gy: 8 (over x_lo, z).
Axes of the slice: x: 4 (x_hi: 2, x_lo: 2; x = x_hi * 2 + x_lo), y: 4, z: 4, core: 2. Of those that a mesh axis runs over, the one named last changes fastest.
Arguments:
- domain_state: float32 [2, 100, 128, 2048], P('group', None, 'gx', 'gy'), may hold values from -4 to 4, as said below
- coupling_field: float32 [2, 128, 2048], P('group', 'gx', 'gy'), may hold values from 0 to 1.5
- regime: int32 [128, 2048], P('gx', 'gy'), may hold values from 0 to 2
- land_class: int32 [100, 128, 2048], P(None, 'gx', 'gy'), may hold values from 0 to 7
- flow_code: int32 [100, 128, 2048], P(None, 'gx', 'gy'), may hold values from 0 to 3, as said below
Outputs:
- domain_out: float32 [2, 100, 128, 2048], P('group', None, 'gx', 'gy')
- coupling_out: float32 [2, 128, 2048], P('group', 'gx', 'gy')
Inputs may be any that keep to these rules, and one draw needn't show every extreme that they name: `domain_state`: slot 0 channels below 50 hold temperatures, the others moisture between 0.2 and 2; slot 1 holds depths between 0.05 and 2. `regime`: 0 warm rain, 1 mixed phase, 2 deep convection. `flow_code`: codes 0, 1, 2, 3 send a cell's outflow to the next column, next row, previous column, previous row.
All inputs are finite; a program needn't handle non-finite values.
Results may differ from a plain program's by a relative error of at most 0.0003.
Values sent between devices are 32-bit elements; how exact they have to be, the bound alone decides.
No kernel may reach another device: no remote copies, remote signals or barrier semaphores. Data moves between devices by JAX's collectives and lax.ppermute only.
A program may use at most 256 MiB of HBM per device.

v0:
```python
import jax
import jax.numpy as jnp
from jax import lax
from jax.sharding import PartitionSpec as P

R = 10
LAYER_TOTAL = 50
STEPS = 4
SUB = 12


def swapped(value, axis, bit):
    mask = 2**bit
    pairs = [(source, source ^ mask) for source in range(lax.axis_size(axis))]
    return lax.ppermute(value, axis, pairs)


def padded_2(shard, sides, width):
    for axis, dim in sides:
        peers, length = (lax.axis_size(axis), shard.shape[dim])
        up = [(i, (i + 1) % peers) for i in range(peers - 1)]
        down = [(j, i) for i, j in up]
        last = lax.slice_in_dim(shard, length - width, length, axis=dim)
        leading = lax.slice_in_dim(shard, 0, width, axis=dim)
        before = lax.ppermute(last, axis, up)
        after = lax.ppermute(leading, axis, down)
        shard = jnp.concatenate([before, shard, after], axis=dim)
    return shard


def atmosphere_step(atmos_profile_state, soil_energy_exchange, regime):
    atmos_thermal_state = atmos_profile_state[:LAYER_TOTAL]
    specific_moisture = atmos_profile_state[LAYER_TOTAL:]
    atmos_thermal_state = jnp.concatenate(
        [atmos_thermal_state[:1] + soil_energy_exchange[None], atmos_thermal_state[1:]], 0
    )
    specific_moisture = jnp.concatenate(
        [specific_moisture[:1] + soil_energy_exchange[None], specific_moisture[1:]], 0
    )
    mixing = jnp.where(regime == 2, 0.4, 0.05)[None].astype(jnp.float32)

    def upward_spreading(profile):
        upper_level = jnp.concatenate([profile[1:], profile[-1:]], 0)
        lower_level = jnp.concatenate([profile[:1], profile[:-1]], 0)
        return profile + mixing * (upper_level + lower_level - 2.0 * profile)

    atmos_thermal_state = upward_spreading(atmos_thermal_state)
    specific_moisture = upward_spreading(specific_moisture)
    layer_number = jnp.arange(LAYER_TOTAL, dtype=jnp.float32)
    moisture_capacity = (0.8 * jnp.exp(-3.0 * layer_number / LAYER_TOTAL))[:, None, None] * jnp.exp(
        0.3 * atmos_thermal_state
    )
    efficiency = jnp.where(regime == 0, 0.3, jnp.where(regime == 1, 0.6, 0.9))[None].astype(
        jnp.float32
    )
    liquid_formed = efficiency * jnp.maximum(specific_moisture - moisture_capacity, 0.0)
    specific_moisture = specific_moisture - liquid_formed
    atmos_thermal_state = atmos_thermal_state + 0.5 * liquid_formed
    rainfall_output = jnp.sum(liquid_formed, axis=0) * (2.0 / LAYER_TOTAL)
    return (jnp.concatenate([atmos_thermal_state, specific_moisture], 0), rainfall_output)


def outflow_of(water_depth, outflow_rate):
    return outflow_rate * water_depth * water_depth / (water_depth + 0.5)


def on_device(domain_state, coupling_field, regime, land_class, flow_code):
    current = domain_state[0]
    incoming = coupling_field[0]
    fine_shape = (R, R) + current.shape[1:]
    land_value = land_class.reshape(fine_shape).astype(jnp.float32)
    outflow_rate = 0.3 + 0.08 * land_value
    keep_share = 1.0 - (0.6 - 0.07 * land_value)
    direction = flow_code.reshape(fine_shape)
    is_route = lax.axis_index("group") == 1
    empty_flux = jnp.zeros(current.shape[1:], jnp.float32)

    def add_rain(atmos_profile_state, rainfall_output):
        water = atmos_profile_state.reshape(fine_shape) + keep_share * rainfall_output[None, None]
        return (water.reshape(atmos_profile_state.shape), empty_flux)

    def run_physics(atmos_profile_state, soil_energy_exchange):
        return atmosphere_step(atmos_profile_state, soil_energy_exchange, regime)

    def edge_outflows(atmos_profile_state):
        water = atmos_profile_state.reshape(fine_shape)
        to_south = jnp.where(
            direction[R - 1] == 1, outflow_of(water[R - 1], outflow_rate[R - 1]), 0.0
        )
        to_north = jnp.where(direction[0] == 3, outflow_of(water[0], outflow_rate[0]), 0.0)
        to_east = jnp.where(
            direction[:, R - 1] == 0, outflow_of(water[:, R - 1], outflow_rate[:, R - 1]), 0.0
        )
        to_west = jnp.where(direction[:, 0] == 2, outflow_of(water[:, 0], outflow_rate[:, 0]), 0.0)
        return jnp.stack([to_south, to_north, to_east, to_west], 0)

    def no_edges(atmos_profile_state):
        return jnp.zeros((4, R) + atmos_profile_state.shape[1:], jnp.float32)

    def apply_flow(atmos_profile_state, from_above, from_below, from_left, from_right):
        water = atmos_profile_state.reshape(fine_shape)
        outflow = outflow_of(water, outflow_rate)
        to_east = jnp.where(direction == 0, outflow, 0.0)
        to_south = jnp.where(direction == 1, outflow, 0.0)
        to_west = jnp.where(direction == 2, outflow, 0.0)
        to_north = jnp.where(direction == 3, outflow, 0.0)
        received = jnp.concatenate([from_above[None], to_south[:-1]], 0)
        received = received + jnp.concatenate([to_north[1:], from_below[None]], 0)
        received = received + jnp.concatenate([from_left[:, None], to_east[:, :-1]], 1)
        received = received + jnp.concatenate([to_west[:, 1:], from_right[:, None]], 1)
        return (water - outflow + received).reshape(atmos_profile_state.shape)

    def keep_column(atmos_profile_state, from_above, from_below, from_left, from_right):
        return atmos_profile_state

    def evaporate(atmos_profile_state):
        water = atmos_profile_state.reshape(fine_shape)
        evaporated = 0.1 * water
        return (
            (water - evaporated).reshape(atmos_profile_state.shape),
            jnp.mean(evaporated, axis=(0, 1)),
        )

    def no_flux(atmos_profile_state):
        return (atmos_profile_state, empty_flux)

    def substep(step_index, atmos_profile_state):
        rim_fields = lax.cond(is_route, edge_outflows, no_edges, atmos_profile_state)
        padded = padded_2(rim_fields, (("gx", 2), ("gy", 3)), 1)
        from_above = padded[0, :, :-2, 1:-1]
        from_below = padded[1, :, 2:, 1:-1]
        from_left = padded[2, :, 1:-1, :-2]
        from_right = padded[3, :, 1:-1, 2:]
        return lax.cond(
            is_route,
            apply_flow,
            keep_column,
            atmos_profile_state,
            from_above,
            from_below,
            from_left,
            from_right,
        )

    for step_index in range(STEPS):
        current, from_physics = lax.cond(is_route, add_rain, run_physics, current, incoming)
        current = lax.fori_loop(0, SUB, substep, current)
        current, from_routing = lax.cond(is_route, evaporate, no_flux, current)
        outgoing = jnp.where(is_route, from_routing, from_physics)
        incoming = swapped(outgoing, "group", 0)
    return (current[None], incoming[None])


def solution(mesh):
    return jax.shard_map(
        on_device,
        mesh=mesh,
        in_specs=(
            P("group", None, "gx", "gy"),
            P("group", "gx", "gy"),
            P("gx", "gy"),
            P(None, "gx", "gy"),
            P(None, "gx", "gy"),
        ),
        out_specs=(P("group", None, "gx", "gy"), P("group", "gx", "gy")),
        check_vma=False,
    )
```

profile of v0, /device:TPU:14, one launch (start us, length us, event | category | flops | bytes accessed | tf_op | source)
XLA Modules:
  0.0 2071.2 jit_solution(9712037584619221253)
XLA Ops:
  7.4 497.9 %while.76 = (s32[]{:T(128)}, f32[100,16,256]{2,1,0:T(8,128)}, pred[]{:T(512)}, s32[10,10,16,256]{3,2,1,0:T(8,128)S(1)}, f32[10,10,16,256]{3,2,1,0:T(8,128)S(1)}, /*index=5*/s32[]{:T(128)}) while((s32[]{:T(128)}, f32[100,16,256]{2,1,0:T(8,128)}, pred[]{:T(512)}, s32[10,10,16,256]{3,2,1,0:T(8,128)S(1)}, f32[10,10,16,256]{3,2,1,0:T(8,128)S(1)}, ...), condition=%wide.region_8.9_spmd, body=%wide.region_3.8_spmd.sunk | while | flops 13213923 | bytes 61404572 | solution.py:147
  517.0 507.2 %while.77 = (s32[]{:T(128)}, f32[100,16,256]{2,1,0:T(8,128)}, pred[]{:T(512)}, s32[10,10,16,256]{3,2,1,0:T(8,128)S(1)}, f32[10,10,16,256]{3,2,1,0:T(8,128)S(1)}, /*index=5*/s32[]{:T(128)}) while((s32[]{:T(128)}, f32[100,16,256]{2,1,0:T(8,128)}, pred[]{:T(512)}, s32[10,10,16,256]{3,2,1,0:T(8,128)S(1)}, f32[10,10,16,256]{3,2,1,0:T(8,128)S(1)}, ...), condition=%wide.region_20.21_spmd, body=%wide.region_15.20_spmd.sunk | while | flops 13213923 | bytes 48297316 | solution.py:147
  549.6 9.6 conditional.35
  591.9 9.6 conditional.35
  634.2 9.6 conditional.35
  676.4 9.6 conditional.35
  718.7 9.6 conditional.35
  761.0 9.6 conditional.35
  803.2 9.6 conditional.35
  845.5 9.6 conditional.35
  887.8 9.6 conditional.35
  930.0 9.6 conditional.35
  972.3 9.6 conditional.35
  1014.6 9.6 conditional.35
  1035.9 507.5 %while.78 = (s32[]{:T(128)}, f32[100,16,256]{2,1,0:T(8,128)}, pred[]{:T(512)}, s32[10,10,16,256]{3,2,1,0:T(8,128)S(1)}, f32[10,10,16,256]{3,2,1,0:T(8,128)S(1)}, /*index=5*/s32[]{:T(128)}) while((s32[]{:T(128)}, f32[100,16,256]{2,1,0:T(8,128)}, pred[]{:T(512)}, s32[10,10,16,256]{3,2,1,0:T(8,128)S(1)}, f32[10,10,16,256]{3,2,1,0:T(8,128)S(1)}, ...), condition=%wide.region_32.33_spmd, body=%wide.region_27.32_spmd.sunk | while | flops 13213923 | bytes 48297316 | solution.py:147
  1068.6 9.6 conditional.37
  1110.9 9.6 conditional.37
  1153.2 9.6 conditional.37
  1195.5 9.6 conditional.37
  1237.8 9.6 conditional.37
  1280.1 9.6 conditional.37
  1322.3 9.6 conditional.37
  1364.6 9.6 conditional.37
  1406.9 9.6 conditional.37
  1449.2 9.6 conditional.37
  1491.5 9.6 conditional.37
  1533.8 9.6 conditional.37
  1555.2 507.2 %while.79 = (s32[]{:T(128)}, f32[100,16,256]{2,1,0:T(8,128)}, pred[]{:T(512)}, s32[10,10,16,256]{3,2,1,0:T(8,128)S(1)}, f32[10,10,16,256]{3,2,1,0:T(8,128)S(1)}, /*index=5*/s32[]{:T(128)}) while((s32[]{:T(128)}, f32[100,16,256]{2,1,0:T(8,128)}, pred[]{:T(512)}, s32[10,10,16,256]{3,2,1,0:T(8,128)S(1)}, f32[10,10,16,256]{3,2,1,0:T(8,128)S(1)}, ...), condition=%wide.region_44.45_spmd, body=%wide.region_39.44_spmd.sunk | while | flops 13213923 | bytes 48297316 | solution.py:147
  1630.1 9.6 conditional.39
  1672.4 9.6 conditional.39
  1714.6 9.6 conditional.39
  1799.2 9.6 conditional.39
  (1362 shorter events, 2413.8 us)
Async XLA Ops:
  20.3 16.2 collective-permute-start.2
  26.5 16.2 collective-permute-start.3
  68.3 16.4 collective-permute-start.3
  110.2 15.4 collective-permute-start.3
  151.2 15.4 collective-permute-start.3
  192.2 15.4 collective-permute-start.3
  233.2 15.4 collective-permute-start.3
  274.2 15.4 collective-permute-start.3
  315.2 15.4 collective-permute-start.3
  356.2 15.4 collective-permute-start.3
  397.1 15.4 collective-permute-start.3
  438.1 15.4 collective-permute-start.3
  479.1 15.4 collective-permute-start.3
  531.8 15.4 collective-permute-start.7
  574.1 15.4 collective-permute-start.7
  616.3 15.4 collective-permute-start.7
  658.6 15.4 collective-permute-start.7
  700.9 15.4 collective-permute-start.7
  743.1 15.4 collective-permute-start.7
  785.4 15.4 collective-permute-start.7
  827.7 15.4 collective-permute-start.7
  869.9 15.4 collective-permute-start.7
  912.2 15.4 collective-permute-start.7
  954.5 15.4 collective-permute-start.7
  996.8 15.4 collective-permute-start.7
  1050.8 15.4 collective-permute-start.11
  1093.1 15.4 collective-permute-start.11
  1135.3 15.4 collective-permute-start.11
  1177.6 15.4 collective-permute-start.11
  1219.9 15.4 collective-permute-start.11
  1262.2 15.4 collective-permute-start.11
  1304.5 15.4 collective-permute-start.11
  (240 other events, 1934.3 us)
where the time goes:
time: 2090 us; the launch traced here: 2070 us
  other arithmetic  703 us (34%)
  waiting for transfers between devices  643 us (31%)
  starting transfers between devices  491 us (23%)
  local copies, waits for them, and re-layouts  228 us (11%)
    ppermute x96, waiting for transfers between devices, padded_2(): before = lax.ppermute(last, axis, up)  334 us
    ppermute x96, starting transfers between devices, padded_2(): before = lax.ppermute(last, axis, up)  302 us
    ppermute x96, waiting for transfers between devices, padded_2(): after = lax.ppermute(leading, axis, down)  288 us
    concatenate x144, other arithmetic, padded_2(): shard = jnp.concatenate([before, shard, after], axis=dim)  246 us
    ppermute x96, starting transfers between devices, padded_2(): after = lax.ppermute(leading, axis, down)  189 us
    add x48, other arithmetic, apply_flow(): return (water - outflow + received).reshape(atmos_profile_state.shape)  154 us
    another operation x96, other arithmetic, edge_outflows(): return jnp.stack([to_south, to_north, to_east, to_west], 0)  94.9 us
    div x48, other arithmetic, outflow_of(): return outflow_rate * water_depth * water_depth / (water_depth + 0.5)  89.6 us
  transfers between devices with their start and end apart: 196, of which 148 were waited for; matrix products, arithmetic and copies ran while one was open for 3% of the time, Pallas kernels for 0%

commit v1 on v0

v1 whole, which is shorter than its diff:
```python
import functools
import math

import jax
import jax.numpy as jnp
from jax import lax
from jax.experimental import pallas as pl
from jax.experimental.pallas import tpu as pltpu
from jax.sharding import PartitionSpec as P

F32 = jnp.float32
R = 10
LEVELS = 50
STEPS = 4
SUB = 12
NX, NY = 16, 256
HALO = STEPS * SUB
OWN = NX * R
ROWS = OWN + 2 * HALO
TILES = ROWS // 8
MAIN = 2 * R
NCH = MAIN + 2
SVR = ROWS + 16
SHARE = MAIN * OWN
EDGE = MAIN * HALO
CH = 2 * LEVELS + 2
SIDE = CH * 48
STATE = CH * 72
FIRST = (0, 1, 3, 4)
GROUP = (8, 10, 13, 8)
VMEM = pltpu.CompilerParams(vmem_limit_bytes=36 * 1024 * 1024)


def rows8(start):
    return pl.ds(start if isinstance(start, int) else pl.multiple_of(start, 8), 8)


def lanes():
    return lax.broadcasted_iota(jnp.int32, (8, 128), 1)


def picked(x, index):
    return jnp.take_along_axis(x, index, axis=1, mode="promise_in_bounds")


def matmul(a, b):
    return lax.dot_general(
        a, b, (((1,), (0,)), ((), ())), precision=lax.Precision.HIGHEST, preferred_element_type=F32
    )


def loop(n, body):
    def step(i, carry):
        body(i)
        return carry

    lax.fori_loop(0, n, step, 0)


def prep_kernel(info, dom, coup, regime, land, flow, own, pay_a, pay_b):
    even = lax.rem(info[1], 2) == 0

    @pl.when(info[0] == 1)
    def _():
        def one(a):
            for b in range(R):
                c = a * R + b
                for h in range(2):
                    cols = slice(128 * h, 128 * h + 128)
                    land_value = land[c, :, cols].astype(F32)
                    code = flow[c, :, cols]
                    rate = 0.3 + 0.08 * land_value
                    keep = 1.0 - (0.6 - 0.07 * land_value)
                    water = dom[c, :, cols] + keep * coup[:, cols]
                    parts = (
                        2.0 * water + 1.0,
                        jnp.where(code == 0, rate, jnp.where(code == 2, -rate, 0.0)),
                        jnp.where(code == 1, rate, jnp.where(code == 3, -rate, 0.0)),
                    )
                    for k, part in enumerate(parts):
                        at = k * SHARE + (h * R + b) * OWN + a
                        own[pl.ds(at, NX, stride=R), :] = part

        loop(R, one)
        low = jnp.where(even, OWN - HALO, 0)

        def rim(i):
            for t in range(HALO // 8):
                pay_a[rows8(i * HALO + 8 * t), :] = own[rows8(i * OWN + low + 8 * t), :]
                pay_b[rows8(i * HALO + 8 * t), :] = own[rows8(i * OWN + OWN - HALO - low + 8 * t), :]

        loop(3 * MAIN, rim)

    @pl.when(info[0] == 0)
    def _():
        def put(c, load):
            for h in range(2):
                top, bottom = load(0, h), load(8, h)
                own[rows8((c * 2 + h) * 16), :] = top
                own[rows8((c * 2 + h) * 16 + 8), :] = bottom
                pay_a[rows8((c * 2 + h) * 8), :] = jnp.where(even, bottom, top)
                pay_b[rows8((c * 2 + h) * 8), :] = jnp.where(even, top, bottom)

        def one(i):
            for u in range(10):
                c = i * 10 + u
                put(c, lambda r, h: dom[c, r : r + 8, 128 * h : 128 * h + 128])

        loop(10, one)
        put(100, lambda r, h: coup[r : r + 8, 128 * h : 128 * h + 128])
        put(101, lambda r, h: regime[r : r + 8, 128 * h : 128 * h + 128].astype(F32))


def strip_maps():
    lane = lanes()
    left = jnp.maximum(lane - 64, 0)
    right = lane + (NY * R - 64)
    return (left % R, left // R), (right % R, jnp.minimum(right // R - 128, 127))


def gathered(sources, column):
    b_of, y_of = column
    out = picked(sources[0], y_of)
    for b in range(1, R):
        out = jnp.where(b_of == b, picked(sources[b], y_of), out)
    return out


def assemble_kernel(info, own, from_a, from_b, st, rate, r02, r13, sr, pay_c, pay_d):
    even_x = lax.rem(info[1], 2) == 0
    even_y = lax.rem(info[2], 2) == 0
    lane = lanes()

    @pl.when(info[0] == 1)
    def _():
        at_a = jnp.where(even_x, ROWS - HALO, 0)
        at_b = ROWS - HALO - at_a

        def one(c):
            for src, n, at in ((own, OWN, HALO), (from_a, HALO, at_a), (from_b, HALO, at_b)):
                for t in range(n // 8):
                    v, h, w = (src[rows8(k * MAIN * n + c * n + 8 * t), :] for k in range(3))
                    to = rows8(c * ROWS + at + 8 * t)
                    st[to, :] = v if src is own else jnp.where(v == 0.0, 1.0, v)
                    r02[to, :] = h
                    r13[to, :] = w
                    rate[to, :] = jnp.abs(h + w)

        loop(MAIN, one)
        left_of, right_of = strip_maps()

        def strips(t):
            for k, src in enumerate((st, r02, r13)):
                found = []
                for half in range(2):
                    at = 8 * t + 128 * half
                    left = gathered([src[rows8(b * ROWS + at), :] for b in range(R)], left_of)
                    right = gathered([src[rows8((R + b) * ROWS + at), :] for b in range(R)], right_of)
                    found.append((left, right))
                    if k == 0:
                        st[rows8(MAIN * ROWS + at), :] = left
                        st[rows8((MAIN + 1) * ROWS + at), :] = right
                    else:
                        sr[rows8(k * 2 * ROWS + at), :] = left
                        sr[rows8(k * 2 * ROWS + ROWS + at), :] = right
                (l0, q0), (l1, q1) = found
                to_left = jnp.where(lane >= 64, l0, pltpu.roll(l1, 64, 1))
                to_right = jnp.where(lane < 64, q0, pltpu.roll(q1, 64, 1))
                pay_c[rows8(k * 128 + 8 * t), :] = jnp.where(even_y, to_right, to_left)
                pay_d[rows8(k * 128 + 8 * t), :] = jnp.where(even_y, to_left, to_right)

        loop(16, strips)

    @pl.when(info[0] == 0)
    def _():
        sub = lax.broadcasted_iota(jnp.int32, (8, 128), 0)

        def one(i):
            for u in range(6):
                j = i * 6 + u
                st[rows8(j * 24), :] = own[rows8(j * 16), :]
                st[rows8(j * 24 + 8), :] = own[rows8(j * 16 + 8), :]
                a, b = from_a[rows8(j * 8), :], from_b[rows8(j * 8), :]
                above, below = jnp.where(even_x, b, a), jnp.where(even_x, a, b)
                st[rows8(j * 24 + 16), :] = jnp.where(sub >= 4, above, below)

        loop(CH * 2 // 6, one)

        def pack(i):
            k, t = i // 3, i % 3
            to_left = jnp.zeros((8, 128), F32)
            to_right = to_left
            for j in range(32):
                c = jnp.minimum(32 * k + j, CH - 1)
                here = (lane >= 4 * j) & (lane < 4 * j + 4)
                west = st[rows8(c * 48 + 8 * t), :]
                east = st[rows8(c * 48 + 24 + 8 * t), :]
                to_left = jnp.where(here, pltpu.roll(west, 4 * j, 1), to_left)
                to_right = jnp.where(here, pltpu.roll(east, (4 * j + 4) % 128, 1), to_right)
            pay_c[rows8(k * 24 + 8 * t), :] = jnp.where(even_y, to_right, to_left)
            pay_d[rows8(k * 24 + 8 * t), :] = jnp.where(even_y, to_left, to_right)

        loop(12, pack)


def atmosphere_column(src, base, stride, flux, regime, put):
    mixing = jnp.where(regime == 2.0, 0.4, 0.05)
    efficiency = jnp.where(regime == 0.0, 0.3, jnp.where(regime == 1.0, 0.6, 0.9))
    load = lambda c: src[rows8(base + c * stride), :]
    heat, damp = load(0) + flux, load(LEVELS) + flux
    heat_below, damp_below = heat, damp
    total = jnp.zeros((8, 128), F32)
    for k in range(LEVELS):
        last = k == LEVELS - 1
        heat_above = heat if last else load(k + 1)
        damp_above = damp if last else load(LEVELS + k + 1)
        t = heat + mixing * (heat_above + heat_below - 2.0 * heat)
        m = damp + mixing * (damp_above + damp_below - 2.0 * damp)
        capacity = (0.8 * math.exp(-3.0 * k / LEVELS)) * jnp.exp(0.3 * t)
        formed = efficiency * jnp.maximum(m - capacity, 0.0)
        put(k, t + 0.5 * formed)
        put(LEVELS + k, m - formed)
        total = total + formed
        heat_below, damp_below, heat, damp = heat, damp, heat_above, damp_above
    return total * (2.0 / LEVELS)


def coarse_row(shape, coarse_dim):
    fine = lax.broadcasted_iota(jnp.int32, shape, 1 - coarse_dim)
    coarse = lax.broadcasted_iota(jnp.int32, shape, coarse_dim)
    of_fine = (fine + 12) // R - 6
    of_coarse = jnp.where(coarse < 20, coarse, coarse - 24)
    return (of_fine == of_coarse).astype(F32)


def lane_map(strip_dim, right, side):
    strip = lax.broadcasted_iota(jnp.int32, (128, 128), strip_dim)
    lane = lax.broadcasted_iota(jnp.int32, (128, 128), 1 - strip_dim)
    column = (strip + (NY * R - 64)) // R if right else (strip + 16) // R - 8
    if side:
        ours = lane < 4 if right else lane >= 124
        column_of = lane + NY if right else lane - 128
        return ((column == column_of) & ours).astype(F32)
    return (column == (lane + 128 if right else lane)).astype(F32)


def route_kernel(step, *refs):
    opening, closing = step == 0, step == STEPS - 1
    if opening:
        info, st, rate, r02, r13, sr_in, from_c, from_d, new, sr, field = refs[:11]
        scratch = refs[11:]
        fld = None
    else:
        info, st, rate, r02, r13, sr, fld, new, field = refs[:9]
        scratch = refs[9:]
    acc, sv0, sv1, rain, sums = scratch
    even_y = lax.rem(info[2], 2) == 0
    lane = lanes()
    first, count, group = FIRST[step], TILES - 2 * FIRST[step], GROUP[step]

    @pl.when(info[0] == 0)
    def _():
        if opening:

            def side(i):
                k, t = i // 3, i % 3
                c, d = from_c[rows8(k * 24 + 8 * t), :], from_d[rows8(k * 24 + 8 * t), :]
                west, east = jnp.where(even_y, d, c), jnp.where(even_y, c, d)
                for j in range(32):
                    block = jnp.where(
                        lane < 4,
                        pltpu.roll(east, (128 - 4 * j) % 128, 1),
                        jnp.where(lane >= 124, pltpu.roll(west, 124 - 4 * j, 1), 0.0),
                    )

                    @pl.when(32 * k + j < CH)
                    def _():
                        st_side[rows8((32 * k + j) * 24 + 8 * t), :] = block

            st_side = acc
            loop(12, side)

        def block(src, dst, base, to, stride, at):
            flux = src[rows8(base + 100 * stride), :] if opening else fld[rows8(at), :]
            regime = src[rows8(base + 101 * stride), :]

            def put(c, value):
                dst[rows8(to + c * stride), :] = value

            put(101, regime)
            field[rows8(at), :] = atmosphere_column(src, base, stride, flux, regime, put)

        if closing:

            def own(i):
                h, t = i // 2, i % 2
                at = h * 24 + 8 * t
                for u in range(2):

                    @pl.when(h == u)
                    def _():
                        cols = slice(128 * u, 128 * u + 128)

                        def put(c, value):
                            new[c, rows8(8 * t), cols] = value

                        field[rows8(8 * t), cols] = atmosphere_column(
                            st, at, 48, fld[rows8(at), :], st[rows8(at + 101 * 48), :], put
                        )

            loop(4, own)
        else:

            def inner(i):
                at = (i // 3) * 24 + 8 * (i % 3)
                block(st, new, at, at, 48, at)

            def outer(t):
                if opening:
                    block(acc, new, 8 * t, SIDE + 8 * t, 24, 48 + 8 * t)
                else:
                    block(st, new, SIDE + 8 * t, SIDE + 8 * t, 24, 48 + 8 * t)

            loop(6, inner)
            loop(3, outer)

    @pl.when(info[0] == 1)
    def _():
        zero = jnp.zeros((8, 128), F32)
        if opening:

            def side(t):
                for half in range(2):
                    at = 8 * t + 128 * half
                    for k in range(3):
                        c, d = from_c[rows8(k * 128 + 8 * t), :], from_d[rows8(k * 128 + 8 * t), :]
                        west, east = jnp.where(even_y, d, c), jnp.where(even_y, c, d)
                        if half:
                            west, east = pltpu.roll(west, 64, 1), pltpu.roll(east, 64, 1)
                        if k == 0:
                            west = jnp.where(west == 0.0, 1.0, west)
                            east = jnp.where(east == 0.0, 1.0, east)
                            left = st[rows8(MAIN * ROWS + at), :]
                            right = st[rows8((MAIN + 1) * ROWS + at), :]
                        else:
                            left = sr_in[rows8(k * 2 * ROWS + at), :]
                            right = sr_in[rows8(k * 2 * ROWS + ROWS + at), :]
                        left = jnp.where(lane >= 64, left, west)
                        right = jnp.where(lane < 64, right, east)
                        if k == 0:
                            acc[rows8(MAIN * ROWS + at), :] = left
                            acc[rows8((MAIN + 1) * ROWS + at), :] = right
                        else:
                            sr[rows8(k * 2 * ROWS + at), :] = left
                            sr[rows8(k * 2 * ROWS + ROWS + at), :] = right
                    for strip in range(2):
                        a = sr[rows8((2 + strip) * ROWS + at), :]
                        b = sr[rows8((4 + strip) * ROWS + at), :]
                        sr[rows8(strip * ROWS + at), :] = jnp.abs(a + b)

            loop(16, side)

        def rate_of(c, at):
            return rate[rows8(c * ROWS + at), :] if c < MAIN else sr[rows8((c - MAIN) * ROWS + at), :]

        def r02_of(c, at):
            return r02[rows8(c * ROWS + at), :] if c < MAIN else sr[rows8((c - MAIN + 2) * ROWS + at), :]

        def r13_of(c, at):
            return r13[rows8(c * ROWS + at), :] if c < MAIN else sr[rows8((c - MAIN + 4) * ROWS + at), :]

        if opening:

            def fill(t):
                at = 8 * t
                for c in range(MAIN):
                    acc[rows8(c * ROWS + at), :] = st[rows8(c * ROWS + at), :]

        else:
            spread = coarse_row((ROWS, 24), 1)
            blocks = [fld[pl.ds(24 * i, 24), :] for i in range(3)]
            sources = (
                blocks[0],
                blocks[1],
                matmul(blocks[0], lane_map(1, False, False)) + matmul(blocks[2], lane_map(1, False, True)),
                matmul(blocks[1], lane_map(1, True, False)) + matmul(blocks[2], lane_map(1, True, True)),
            )
            for i, source in enumerate(sources):
                rain[pl.ds(i * ROWS, ROWS), :] = matmul(spread, source)

            def fill(t):
                at = 8 * (t + first)
                for c in range(NCH):
                    fall = rain[rows8((c // R if c < MAIN else c - MAIN + 2) * ROWS + at), :]
                    share = 0.275 + 1.75 * rate_of(c, at)
                    acc[rows8(c * ROWS + at), :] = st[rows8(c * ROWS + at), :] + share * fall

        loop(count, fill)

        def clear(t):
            for c in range(NCH):
                sv0[rows8(c * SVR + 8 * (t + first)), :] = zero

        loop(count + 2, clear)
        for c in range(NCH):
            sv1[rows8(c * SVR + 8 * first), :] = zero
            sv1[rows8(c * SVR + 8 * (first + count + 1)), :] = zero

        at_first, at_last = lane == 0, lane == 127

        def settled(sv, c, at):
            row = c * SVR + 8 + at
            above = jnp.maximum(sv[pl.ds(row - 1, 8), :], 0.0)
            below = jnp.minimum(sv[pl.ds(row + 1, 8), :], 0.0)
            return acc[rows8(c * ROWS + at), :] + above - below

        def substep(sv_in, sv_out, i):
            for g in range(group):
                at = 8 * (first + g) + i * (8 * group)

                def cell(c):
                    v = settled(sv_in, c, at)
                    q = (v - 2.0) + pltpu.reciprocal(v, approx=True)
                    sv_out[rows8(c * SVR + 8 + at), :] = r13_of(c, at) * q
                    return v - rate_of(c, at) * q, r02_of(c, at) * q

                heads = [cell(h * R) for h in range(2)]
                tails = [cell(h * R + R - 1) for h in range(2)]
                east = [pltpu.roll(jnp.maximum(x[1], 0.0), 1, 1) for x in tails]
                west = [pltpu.roll(jnp.minimum(x[1], 0.0), 127, 1) for x in heads]
                for c in (MAIN, MAIN + 1):
                    kept, across = cell(c)
                    kept = kept + pltpu.roll(jnp.maximum(across, 0.0), 1, 1)
                    acc[rows8(c * ROWS + at), :] = kept - pltpu.roll(jnp.minimum(across, 0.0), 127, 1)
                for h in range(2):
                    this = heads[h]
                    value = this[0] + jnp.where(at_first, east[1 - h], east[h])
                    for b in range(1, R):
                        after = cell(h * R + b) if b < R - 1 else tails[h]
                        acc[rows8((h * R + b - 1) * ROWS + at), :] = value - jnp.minimum(after[1], 0.0)
                        value = after[0] + jnp.maximum(this[1], 0.0)
                        this = after
                    acc[rows8((h * R + R - 1) * ROWS + at), :] = value - jnp.where(
                        at_last, west[1 - h], west[h]
                    )

        def pair(_):
            loop(count // group, functools.partial(substep, sv0, sv1))
            loop(count // group, functools.partial(substep, sv1, sv0))

        loop(SUB // 2, pair)

        left_of, right_of = strip_maps()
        start = HALO // 8 if closing else FIRST[step + 1]
        for i in range(4 * TILES):
            if not start <= i % TILES < TILES - start:
                sums[rows8(8 * i), :] = zero

        def finish(t):
            at = 8 * (t + start)
            v = [settled(sv0, c, at) for c in range(NCH)]
            for b in range(R):
                place = 10 * lane + b
                inner = jnp.clip(place + 64, 0, 127)
                v[b] = jnp.where(place < SUB, picked(v[MAIN], inner), v[b])
                place = place - (R * 128 - 64)
                inner = jnp.clip(place, 0, 127)
                v[R + b] = jnp.where(place >= 64 - SUB, picked(v[MAIN + 1], inner), v[R + b])
            for h in range(2):
                total = v[h * R]
                for b in range(1, R):
                    total = total + v[h * R + b]
                sums[rows8(h * ROWS + at), :] = total - float(R)
            if not closing:
                v[MAIN] = jnp.where(lane >= 64 + SUB, gathered(v[:R], left_of), v[MAIN])
                v[MAIN + 1] = jnp.where(lane < 64 - SUB, gathered(v[R:MAIN], right_of), v[MAIN + 1])
                sums[rows8(2 * ROWS + at), :] = v[MAIN] - 1.0
                sums[rows8(3 * ROWS + at), :] = v[MAIN + 1] - 1.0
                for c in range(NCH):
                    new[rows8(c * ROWS + at), :] = 0.9 * v[c] + 0.1
            else:
                for c in range(MAIN):
                    acc[rows8(c * ROWS + at), :] = 0.45 * (v[c] - 1.0)

        loop(TILES - 2 * start, finish)
        pool = coarse_row((24, ROWS), 0)
        parts = [matmul(pool, sums[pl.ds(i * ROWS, ROWS), :]) for i in range(2 if closing else 4)]
        scale = 0.1 / (2.0 * R * R)
        if closing:
            for h in range(2):
                field[:, 128 * h : 128 * h + 128] = parts[h][:NX] * scale

            def lay(a):
                for b in range(R):
                    for h in range(2):
                        new[a * R + b, :, 128 * h : 128 * h + 128] = acc[
                            pl.ds((h * R + b) * ROWS + HALO + a, NX, stride=R), :
                        ]

            loop(R, lay)
        else:
            field[pl.ds(0, 24), :] = parts[0] * scale
            field[pl.ds(24, 24), :] = parts[1] * scale
            side_part = matmul(parts[2], lane_map(0, False, True)) + matmul(parts[3], lane_map(0, True, True))
            field[pl.ds(48, 24), :] = side_part * scale


def shapes(*sizes):
    return [jax.ShapeDtypeStruct(s if isinstance(s, tuple) else (s, 128), F32) for s in sizes]


def call(kernel, args, out, scratch=()):
    in_specs = [pl.BlockSpec(memory_space=pltpu.SMEM)]
    in_specs += [pl.BlockSpec(memory_space=pltpu.VMEM)] * (len(args) - 1)
    return pl.pallas_call(
        kernel,
        out_shape=shapes(*out),
        in_specs=in_specs,
        out_specs=[pl.BlockSpec(memory_space=pltpu.VMEM)] * len(out),
        scratch_shapes=[pltpu.VMEM((n, 128), F32) for n in scratch],
        compiler_params=VMEM,
    )(*args)


def pairs(axis, odd):
    n = lax.axis_size(axis)
    found = [(i, i + 1) for i in range(odd, n - 1, 2)]
    return found + [(j, i) for i, j in found]


def on_device(domain_state, coupling_field, regime, land_class, flow_code):
    info = jnp.stack([lax.axis_index(a) for a in ("group", "gx", "gy")]).astype(jnp.int32)
    args = (info, domain_state[0], coupling_field[0], regime, land_class, flow_code)
    own, pay_a, pay_b = call(prep_kernel, args, (3 * SHARE, 3 * EDGE, 3 * EDGE))
    from_a = lax.ppermute(pay_a, "gx", pairs("gx", 0))
    from_b = lax.ppermute(pay_b, "gx", pairs("gx", 1))
    full = MAIN * ROWS
    st, rate, r02, r13, sr, pay_c, pay_d = call(
        assemble_kernel,
        (info, own, from_a, from_b),
        (STATE, full, full, full, 6 * ROWS, 384, 384),
    )
    from_c = lax.ppermute(pay_c, "gy", pairs("gy", 0))
    from_d = lax.ppermute(pay_d, "gy", pairs("gy", 1))
    scratch = (NCH * ROWS, NCH * SVR, NCH * SVR, 4 * ROWS, 4 * ROWS)
    for step in range(STEPS):
        kernel = functools.partial(route_kernel, step)
        if step == 0:
            st, sr, field = call(
                kernel, (info, st, rate, r02, r13, sr, from_c, from_d), (STATE, 6 * ROWS, 72), scratch
            )
        elif step < STEPS - 1:
            st, field = call(kernel, (info, st, rate, r02, r13, sr, field), (STATE, 72), scratch)
        else:
            out, field = call(
                kernel,
                (info, st, rate, r02, r13, sr, field),
                ((2 * LEVELS, NX, NY), (NX, NY)),
                scratch,
            )
        field = lax.ppermute(field, "group", [(0, 1), (1, 0)])
    return (out[None], field[None])


def solution(mesh):
    return jax.shard_map(
        on_device,
        mesh=mesh,
        in_specs=(
            P("group", None, "gx", "gy"),
            P("group", "gx", "gy"),
            P("gx", "gy"),
            P(None, "gx", "gy"),
            P(None, "gx", "gy"),
        ),
        out_specs=(P("group", None, "gx", "gy"), P("group", "gx", "gy")),
        check_vma=False,
    )
```

time: 2090 us -> 190 us (0.09)
  other arithmetic: 703 us -> 0.08 us
  waiting for transfers between devices: 643 us -> 46.2 us
  starting transfers between devices: 491 us -> 9.12 us
  local copies, waits for them, and re-layouts: 228 us -> 8.54 us
  Pallas kernels: 0 us -> 125 us
    ppermute x196 -> x8, waiting for transfers between devices: 643 us -> 46.2 us  [the longest x4 21.7 us: on_device(): field = lax.ppermute(field, 'group', [(0, 1), (1, 0)])]
    ppermute x196 -> x8, starting transfers between devices: 491 us -> 9.12 us  [the longest x1 4.68 us: on_device(): from_d = lax.ppermute(pay_d, 'gy', pairs('gy', 1))]
    concatenate x144 -> x0, other arithmetic: 246 us -> none  [padded_2(): shard = jnp.concatenate([before, shard, after], axis=dim)]
    add x53 -> x0, other arithmetic: 170 us -> none  [the longest x48 154 us: apply_flow(): return (water - outflow + received).reshape(atmos_profile_state.shape)]
    slice x192 -> x0, local copies, waits for them, and re-layouts: 155 us -> none  [the longest x96 63.5 us: padded_2(): leading = lax.slice_in_dim(shard, 0, width, axis=dim)]
    pallas_call x0 -> x6, Pallas kernels: none -> 125 us  [call(): pl.pallas_call(kernel, out_shape=shapes(*out), in_specs=in_specs, out_spe...]
    another operation x96 -> x1, other arithmetic: 94.9 us -> 0.08 us  [on_device(): jnp.stack([lax.axis_index(a) for a in ('group', 'gx', 'gy')])]
    select_n x148 -> x0, other arithmetic: 91.3 us -> none  [the longest x48 52.7 us: edge_outflows(): jnp.where(direction[:, R - 1] == 0, outflow_of(water[:, R - 1], outflow_r...]
  transfers between devices with their start and end apart: 196 -> 8, of which waited for: 148 -> 8; matrix products, arithmetic and copies ran while one was open for 3% -> 0% of each run, Pallas kernels for 0% -> 0%
where the time goes in v1:
time: 190 us
  Pallas kernels  125 us (66%)
  waiting for transfers between devices  46.2 us (24%)
  starting transfers between devices  9.12 us (5%)
  local copies, waits for them, and re-layouts  8.54 us (4%)
    pallas_call x6, Pallas kernels, call(): pl.pallas_call(kernel, out_shape=shapes(*out), in_specs=in_specs, out_spe...  125 us
    ppermute x4, waiting for transfers between devices, on_device(): field = lax.ppermute(field, 'group', [(0, 1), (1, 0)])  21.7 us
    ppermute x1, waiting for transfers between devices, on_device(): from_b = lax.ppermute(pay_b, 'gx', pairs('gx', 1))  17.4 us
    unnamed x13, local copies, waits for them, and re-layouts  8.54 us
    ppermute x1, waiting for transfers between devices, on_device(): from_d = lax.ppermute(pay_d, 'gy', pairs('gy', 1))  5.45 us
    ppermute x1, starting transfers between devices, on_device(): from_d = lax.ppermute(pay_d, 'gy', pairs('gy', 1))  4.68 us
  transfers between devices with their start and end apart: 8, of which 8 were waited for; matrix products, arithmetic and copies ran while one was open for 0% of the time, Pallas kernels for 0%

profile of v1, /device:TPU:14, one launch (start us, length us, event | category | flops | bytes accessed | tf_op | source)
XLA Modules:
  0.0 189.7 jit_solution(13939331960759465949)
XLA Ops:
  0.6 0.1 pad_add_fusion.info.refs_0_
  0.7 0.0 copy-start.1
  0.7 1.4 copy-done.1
  2.1 1.4 copy-done.2
  3.6 1.4 copy-done.3
  5.0 0.7 copy-done.4
  5.7 0.7 copy-done.5
  6.4 2.1 %shard_map.68 = (f32[9600,128]{1,0:T(8,128)S(1)}, f32[2880,128]{1,0:T(8,128)S(1)}, f32[2880,128]{1,0:T(8,128)S(1)}) custom-call(s32[3]{0:T(128)S(1)} %pad_add_fusion.info.refs_0_, f32[100,16,256]{2,1,0:T(8,128)S(1)} %bitcast.7, f32[16,256]{1,0:T(8,128)S(1)} %bitcast.8, s32[16,256]{1,0:T(8,128)S(1)} %copy-done.5, s32[100,16,256]{2,1,0:T(8,128)S(1)} %copy-done.2, ...), custom_call_target="tpu_custom_call" | custom-call | tf_op jit(solution)/shard_map/pallas_call | solution.py:515
  8.6 0.0 copy-start
  8.6 2.2 %copy-done = f32[9600,128]{1,0:T(8,128)} copy-done((f32[9600,128]{1,0:T(8,128)}, f32[9600,128]{1,0:T(8,128)S(1)}, u32[]{:S(2)}) %copy-start) | copy-done | bytes 4915224
  10.8 0.0 collective-permute-start
  10.8 2.5 %collective-permute-start.1 = (f32[2880,128]{1,0:T(8,128)S(1)}, f32[2880,128]{1,0:T(8,128)S(1)}, u32[]{:S(2)}, u32[]{:S(2)}) collective-permute-start(f32[2880,128]{1,0:T(8,128)S(1)} %get-tuple-element.23), channel_id=1, source_target_pairs={{8,16},{24,32},{40,48},{16,8},{32,24},{48,40},{9,17},{25,33},{41,4... | collective-permute-start | bytes 4423688 | tf_op jit(solution)/shard_map/ppermute | solution.py:536
  13.2 0.8 collective-permute-done.from_a
  14.0 17.4 %collective-permute-done.1.from_b = f32[2880,128]{1,0:T(8,128)S(1)} collective-permute-done((f32[2880,128]{1,0:T(8,128)S(1)}, f32[2880,128]{1,0:T(8,128)S(1)}, u32[]{:S(2)}, u32[]{:S(2)}) %collective-permute-start.1) | collective-permute-done | bytes 1474592 | tf_op jit(solution)/shard_map/ppermute | solution.py:536
  31.5 9.1 %shard_map.69 = (f32[7344,128]{1,0:T(8,128)S(1)}, f32[5120,128]{1,0:T(8,128)S(1)}, f32[5120,128]{1,0:T(8,128)S(1)}, f32[5120,128]{1,0:T(8,128)S(1)}, f32[1536,12...) custom-call(s32[3]{0:T(128)S(1)} %pad_add_fusion.info.refs_0_, f32[9600,128]{1,0:T(8,128)} %copy-done, ...), custom_call_target="tpu_custom_call" | custom-call | tf_op jit(solution)/shard_map/pallas_call | solution.py:515
  40.6 2.0 %collective-permute-start.2 = (f32[384,128]{1,0:T(8,128)S(1)}, f32[384,128]{1,0:T(8,128)S(1)}, u32[]{:S(2)}, u32[]{:S(2)}) collective-permute-start(f32[384,128]{1,0:T(8,128)S(1)} %get-tuple-element.29), channel_id=1, source_target_pairs={{0,1},{2,3},{4,5},{6,7},{1,0},{3,2},{5,4},{7,6},{8,9},{10,11},{12,... | collective-permute-start | bytes 589832 | tf_op jit(solution)/shard_map/ppermute | solution.py:543
  42.6 4.7 %collective-permute-start.3 = (f32[384,128]{1,0:T(8,128)S(1)}, f32[384,128]{1,0:T(8,128)S(1)}, u32[]{:S(2)}, u32[]{:S(2)}) collective-permute-start(f32[384,128]{1,0:T(8,128)S(1)} %get-tuple-element.30), channel_id=1, source_target_pairs={{1,2},{3,4},{5,6},{2,1},{4,3},{6,5},{9,10},{11,12},{13,14},{10,9},... | collective-permute-start | bytes 589832 | tf_op jit(solution)/shard_map/ppermute | solution.py:544
  47.2 0.9 collective-permute-done.2.refs_6_
  48.1 5.5 %collective-permute-done.3.refs_7_ = f32[384,128]{1,0:T(8,128)S(1)} collective-permute-done((f32[384,128]{1,0:T(8,128)S(1)}, f32[384,128]{1,0:T(8,128)S(1)}, u32[]{:S(2)}, u32[]{:S(2)}) %collective-permute-start.3) | collective-permute-done | bytes 196640 | tf_op jit(solution)/shard_map/ppermute | solution.py:544
  53.6 32.9 %shard_map.70 = (f32[7344,128]{1,0:T(8,128)S(1)}, f32[1536,128]{1,0:T(8,128)S(1)}, f32[72,128]{1,0:T(8,128)S(1)}) custom-call(s32[3]{0:T(128)S(1)} %pad_add_fusion.info.refs_0_, f32[7344,128]{1,0:T(8,128)S(1)} %get-tuple-element.24.refs_1_, f32[5120,128]{1,0:T(8,128)S(1)} %get-tuple-element.25.refs_2_, f32[5120,128]{1,0:T(8,128)S(1)} %get-tuple-element.26.refs_3_, ...), custom_call_target="tpu_custom_call" | custom-call | tf_op jit(solution)/shard_map/pallas_call | solution.py:515
  86.5 0.0 collective-permute-start.4
  86.5 5.5 %collective-permute-done.4.refs_6_ = f32[72,128]{1,0:T(8,128)S(1)} collective-permute-done((f32[72,128]{1,0:T(8,128)S(1)}, f32[72,128]{1,0:T(8,128)S(1)}, u32[]{:S(2)}, u32[]{:S(2)}) %collective-permute-start.4) | collective-permute-done | bytes 36896 | tf_op jit(solution)/shard_map/ppermute | solution.py:561
  91.9 30.2 %shard_map.71 = (f32[7344,128]{1,0:T(8,128)S(1)}, f32[72,128]{1,0:T(8,128)S(1)}) custom-call(s32[3]{0:T(128)S(1)} %pad_add_fusion.info.refs_0_, f32[7344,128]{1,0:T(8,128)S(1)} %get-tuple-element.31.refs_1_, f32[5120,128]{1,0:T(8,128)S(1)} %get-tuple-element.25.refs_2_, f32[5120,128]{1,0:T(8,128)S(1)} %get-tuple-element.26.refs_3_, ...), custom_call_target="tpu_custom_call" | custom-call | tf_op jit(solution)/shard_map/pallas_call | solution.py:515
  122.2 0.0 collective-permute-start.5
  122.2 5.5 %collective-permute-done.5.refs_6_ = f32[72,128]{1,0:T(8,128)S(1)} collective-permute-done((f32[72,128]{1,0:T(8,128)S(1)}, f32[72,128]{1,0:T(8,128)S(1)}, u32[]{:S(2)}, u32[]{:S(2)}) %collective-permute-start.5) | collective-permute-done | bytes 36896 | tf_op jit(solution)/shard_map/ppermute | solution.py:561
  127.6 27.0 %shard_map.72 = (f32[7344,128]{1,0:T(8,128)S(1)}, f32[72,128]{1,0:T(8,128)S(1)}) custom-call(s32[3]{0:T(128)S(1)} %pad_add_fusion.info.refs_0_, f32[7344,128]{1,0:T(8,128)S(1)} %get-tuple-element.34.refs_1_, f32[5120,128]{1,0:T(8,128)S(1)} %get-tuple-element.25.refs_2_, f32[5120,128]{1,0:T(8,128)S(1)} %get-tuple-element.26.refs_3_, ...), custom_call_target="tpu_custom_call" | custom-call | tf_op jit(solution)/shard_map/pallas_call | solution.py:515
  154.6 0.0 collective-permute-start.6
  154.6 5.5 %collective-permute-done.6.refs_6_ = f32[72,128]{1,0:T(8,128)S(1)} collective-permute-done((f32[72,128]{1,0:T(8,128)S(1)}, f32[72,128]{1,0:T(8,128)S(1)}, u32[]{:S(2)}, u32[]{:S(2)}) %collective-permute-start.6) | collective-permute-done | bytes 36896 | tf_op jit(solution)/shard_map/ppermute | solution.py:561
  160.1 23.7 %shard_map.73 = (f32[100,16,256]{2,1,0:T(8,128)}, f32[16,256]{1,0:T(8,128)S(1)}) custom-call(s32[3]{0:T(128)S(1)} %pad_add_fusion.info.refs_0_, f32[7344,128]{1,0:T(8,128)S(1)} %get-tuple-element.36.refs_1_, f32[5120,128]{1,0:T(8,128)S(1)} %get-tuple-element.25.refs_2_, f32[5120,128]{1,0:T(8,128)S(1)} %get-tuple-element.26.refs_3_, ...), custom_call_target="tpu_custom_call" | custom-call | tf_op jit(solution)/shard_map/pallas_call | solution.py:515
  183.8 0.0 collective-permute-start.7
  183.8 5.2 %collective-permute-done.7 = f32[16,256]{1,0:T(8,128)S(1)} collective-permute-done((f32[16,256]{1,0:T(8,128)S(1)}, f32[16,256]{1,0:T(8,128)S(1)}, u32[]{:S(2)}, u32[]{:S(2)}) %collective-permute-start.7) | collective-permute-done | bytes 16416 | tf_op jit(solution)/shard_map/ppermute | solution.py:561
  189.0 0.6 copy.8
  (4 shorter events, 0.0 us)
Async XLA Ops:
  0.7 1.4 copy-start.1
  2.1 1.4 copy-start.2
  3.6 1.4 copy-start.3
  5.0 0.7 copy-start.4
  5.7 0.7 copy-start.5
  8.6 2.2 %copy-start = (f32[9600,128]{1,0:T(8,128)}, f32[9600,128]{1,0:T(8,128)S(1)}, u32[]{:S(2)}) copy-start(f32[9600,128]{1,0:T(8,128)S(1)} %get-tuple-element.21.own) | copy-start | bytes 14745604
  10.8 3.3 %collective-permute-start = (f32[2880,128]{1,0:T(8,128)S(1)}, f32[2880,128]{1,0:T(8,128)S(1)}, u32[]{:S(2)}, u32[]{:S(2)}) collective-permute-start(f32[2880,128]{1,0:T(8,128)S(1)} %get-tuple-element.22), channel_id=1, source_target_pairs={{0,8},{16,24},{32,40},{48,56},{8,0},{24,16},{40,32},{56,48},{1,9},... | collective-permute-start | bytes 4423688 | tf_op jit(solution)/shard_map/ppermute | solution.py:535
  10.8 20.7 %collective-permute-start.1 = (f32[2880,128]{1,0:T(8,128)S(1)}, f32[2880,128]{1,0:T(8,128)S(1)}, u32[]{:S(2)}, u32[]{:S(2)}) collective-permute-start(f32[2880,128]{1,0:T(8,128)S(1)} %get-tuple-element.23), channel_id=1, source_target_pairs={{8,16},{24,32},{40,48},{16,8},{32,24},{48,40},{9,17},{25,33},{41,4... | collective-permute-start | bytes 4423688 | tf_op jit(solution)/shard_map/ppermute | solution.py:536
  40.6 7.5 %collective-permute-start.2 = (f32[384,128]{1,0:T(8,128)S(1)}, f32[384,128]{1,0:T(8,128)S(1)}, u32[]{:S(2)}, u32[]{:S(2)}) collective-permute-start(f32[384,128]{1,0:T(8,128)S(1)} %get-tuple-element.29), channel_id=1, source_target_pairs={{0,1},{2,3},{4,5},{6,7},{1,0},{3,2},{5,4},{7,6},{8,9},{10,11},{12,... | collective-permute-start | bytes 589832 | tf_op jit(solution)/shard_map/ppermute | solution.py:543
  42.6 11.0 %collective-permute-start.3 = (f32[384,128]{1,0:T(8,128)S(1)}, f32[384,128]{1,0:T(8,128)S(1)}, u32[]{:S(2)}, u32[]{:S(2)}) collective-permute-start(f32[384,128]{1,0:T(8,128)S(1)} %get-tuple-element.30), channel_id=1, source_target_pairs={{1,2},{3,4},{5,6},{2,1},{4,3},{6,5},{9,10},{11,12},{13,14},{10,9},... | collective-permute-start | bytes 589832 | tf_op jit(solution)/shard_map/ppermute | solution.py:544
  86.5 5.5 %collective-permute-start.4 = (f32[72,128]{1,0:T(8,128)S(1)}, f32[72,128]{1,0:T(8,128)S(1)}, u32[]{:S(2)}, u32[]{:S(2)}) collective-permute-start(f32[72,128]{1,0:T(8,128)S(1)} %get-tuple-element.33), channel_id=1, source_target_pairs={{0,64},{64,0},{1,65},{65,1},{2,66},{66,2},{3,67},{67,3},{4,68},{68... | collective-permute-start | bytes 110600 | tf_op jit(solution)/shard_map/ppermute | solution.py:561
  122.2 5.5 %collective-permute-start.5 = (f32[72,128]{1,0:T(8,128)S(1)}, f32[72,128]{1,0:T(8,128)S(1)}, u32[]{:S(2)}, u32[]{:S(2)}) collective-permute-start(f32[72,128]{1,0:T(8,128)S(1)} %get-tuple-element.35), channel_id=1, source_target_pairs={{0,64},{64,0},{1,65},{65,1},{2,66},{66,2},{3,67},{67,3},{4,68},{68... | collective-permute-start | bytes 110600 | tf_op jit(solution)/shard_map/ppermute | solution.py:561
  154.6 5.5 %collective-permute-start.6 = (f32[72,128]{1,0:T(8,128)S(1)}, f32[72,128]{1,0:T(8,128)S(1)}, u32[]{:S(2)}, u32[]{:S(2)}) collective-permute-start(f32[72,128]{1,0:T(8,128)S(1)} %get-tuple-element.37), channel_id=1, source_target_pairs={{0,64},{64,0},{1,65},{65,1},{2,66},{66,2},{3,67},{67,3},{4,68},{68... | collective-permute-start | bytes 110600 | tf_op jit(solution)/shard_map/ppermute | solution.py:561
  183.8 5.2 %collective-permute-start.7 = (f32[16,256]{1,0:T(8,128)S(1)}, f32[16,256]{1,0:T(8,128)S(1)}, u32[]{:S(2)}, u32[]{:S(2)}) collective-permute-start(f32[16,256]{1,0:T(8,128)S(1)} %get-tuple-element.39), channel_id=1, source_target_pairs={{0,64},{64,0},{1,65},{65,1},{2,66},{66,2},{3,67},{67,3},{4,68},{68... | collective-permute-start | bytes 49160 | tf_op jit(solution)/shard_map/ppermute | solution.py:561

commit v2 on v1

v2 whole, which is shorter than its diff:
```python
import functools
import math

import jax
import jax.numpy as jnp
from jax import lax
from jax.experimental import pallas as pl
from jax.experimental.pallas import tpu as pltpu
from jax.sharding import PartitionSpec as P

F32 = jnp.float32
R = 10
LEVELS = 50
STEPS = 4
SUB = 12
NX, NY = 16, 256
HALO = STEPS * SUB
OWN = NX * R
ROWS = OWN + 2 * HALO
TILES = ROWS // 8
MAIN = 2 * R
NCH = MAIN + 2
SVR = ROWS + 16
EDGE = MAIN * HALO
CH = 2 * LEVELS + 2
RANGES = (
    ((0, 8, 12),),
    ((1, 10, 4), (2, 14, 8)),
    ((3, 13, 8), (4, 8, 4)),
    ((4, 8, 4), (5, 11, 8)),
)
MIB = 1024 * 1024
EDGE_TILES = 9


def rows8(start):
    return pl.ds(start if isinstance(start, int) else pl.multiple_of(start, 8), 8)


def lanes():
    return lax.broadcasted_iota(jnp.int32, (8, 128), 1)


def picked(x, index):
    return jnp.take_along_axis(x, index, axis=1, mode="promise_in_bounds")


def loop(n, body):
    def step(i, carry):
        body(i)
        return carry

    lax.fori_loop(0, n, step, 0)


def info_of():
    return [lax.axis_index(a) for a in ("group", "gx", "gy")]


class Inputs:
    def __init__(self, hbm, vmem, sems, sems2):
        self.dom, self.coup, self.regime, self.land, self.flow = vmem
        self.big = [(hbm[i], vmem[i]) for i in (0, 3, 4)]
        self.small = [pltpu.make_async_copy(hbm[i], vmem[i], sems2.at[i - 1]) for i in (1, 2)]
        self.sems = sems

    def part(self, k, i):
        src, dst = self.big[k]
        cut = pl.ds(i * R, R)
        return pltpu.make_async_copy(src.at[cut], dst.at[cut], self.sems.at[k, i])

    def start(self, kinds):
        for x in self.small:
            x.start()
        for i in range(R):
            for k in range(kinds):
                self.part(k, i).start()
        for x in self.small:
            x.wait()

    def wait(self, kinds, i):
        for k in range(kinds):
            self.part(k, i).wait()

    def lay_out(self, put):
        self.start(3)

        def one(a):
            self.wait(3, a)
            for b in range(R):
                c = a * R + b
                for h in range(2):
                    cols = slice(128 * h, 128 * h + 128)
                    land_value = self.land[c, :, cols].astype(F32)
                    code = self.flow[c, :, cols]
                    rate = 0.3 + 0.08 * land_value
                    keep = 1.0 - (0.6 - 0.07 * land_value)
                    water = self.dom[c, :, cols] + keep * self.coup[:, cols]
                    put(0, h * R + b, a, 2.0 * water + 1.0)
                    put(1, h * R + b, a, jnp.where(code == 0, rate, jnp.where(code == 2, -rate, 0.0)))
                    put(2, h * R + b, a, jnp.where(code == 1, rate, jnp.where(code == 3, -rate, 0.0)))

        loop(R, one)

    def blocks(self, put):
        self.start(1)

        def one(i):
            self.wait(1, i)
            for u in range(10):
                for h in range(2):
                    for t in range(2):
                        put(i * 10 + u, h, t, self.dom[i * 10 + u, 8 * t : 8 * t + 8, 128 * h : 128 * h + 128])

        loop(R, one)
        for h in range(2):
            for t in range(2):
                cut = (slice(8 * t, 8 * t + 8), slice(128 * h, 128 * h + 128))
                put(100, h, t, self.coup[cut])
                put(101, h, t, self.regime[cut].astype(F32))


def prep_kernel(*refs):
    pay_a, pay_b, own = refs[5], refs[6], refs[14]
    inputs = Inputs(refs[:5], refs[7:12], *refs[12:14])
    group, gx, _ = info_of()
    even = lax.rem(gx, 2) == 0

    @pl.when(group == 1)
    def _():
        def put(k, c, a, value):
            own[k * MAIN + c, pl.ds(a, NX, stride=R), :] = value

        inputs.lay_out(put)
        low = jnp.where(even, OWN - HALO, 0)

        def rim(i):
            for t in range(HALO // 8):
                pay_a[rows8(i * HALO + 8 * t), :] = own[i, rows8(low + 8 * t), :]
                pay_b[rows8(i * HALO + 8 * t), :] = own[i, rows8(OWN - HALO - low + 8 * t), :]

        loop(3 * MAIN, rim)

    @pl.when(group == 0)
    def _():
        def put(c, h, t, value):
            @pl.when(even == (t == 1))
            def _():
                pay_a[rows8((c * 2 + h) * 8), :] = value

            @pl.when(even == (t == 0))
            def _():
                pay_b[rows8((c * 2 + h) * 8), :] = value

        inputs.blocks(put)


def early_kernel(*refs):
    stw, sta, r02, r13, inner = refs[5:10]
    inputs = Inputs(refs[:5], refs[10:15], *refs[15:17])
    acc, sv0, sv1 = refs[17:]
    group, _, _ = info_of()

    @pl.when(group == 1)
    def _():
        def put(k, c, a, value):
            (stw, r02, r13)[k][c, pl.ds(HALO + a, NX, stride=R), :] = value

        inputs.lay_out(put)
        begin, size = HALO // 8, 10

        def fill(t):
            here = rows8(8 * (t + begin))
            for c in range(MAIN):
                acc[c, here, :] = stw[c, here, :]

        loop(OWN // 8, fill)
        zero = jnp.zeros((8, 128), F32)

        def clear(t):
            for c in range(MAIN):
                sv0[c, rows8(8 * (t + begin)), :] = zero

        loop(OWN // 8 + 2, clear)
        for c in range(MAIN):
            sv1[c, rows8(8 * begin), :] = zero
            sv1[c, rows8(HALO + OWN + 8), :] = zero
        flow = Flow(acc, lambda k, c, here: (r02, r13)[k][c, here, :])

        def pair(_):
            loop(OWN // (8 * size), functools.partial(flow.substep, begin, size, sv0, sv1, range(2), ()))
            loop(OWN // (8 * size), functools.partial(flow.substep, begin, size, sv1, sv0, range(2), ()))

        loop(SUB // 2, pair)

        def finish(t):
            for u in range(2):
                at = 16 * t + HALO + 8 * u
                for c in range(MAIN):
                    inner[c, rows8(at), :] = flow.settled(sv0, c, at)

        loop(OWN // 16, finish)

    @pl.when(group == 0)
    def _():
        def put(c, h, t, value):
            sta[c, 24 * h + 8 * t : 24 * h + 8 * t + 8, :] = value

        inputs.blocks(put)


class Flow:
    def __init__(self, acc, rate):
        self.acc, self.rate = acc, rate

    def settled(self, sv, c, at):
        above = jnp.maximum(sv[c, pl.ds(at + 7, 8), :], 0.0)
        below = jnp.minimum(sv[c, pl.ds(at + 9, 8), :], 0.0)
        return self.acc[c, rows8(at), :] + above - below

    def substep(self, begin, group, sv_in, sv_out, halves, strips, i):
        acc, lane = self.acc, lanes()
        start = pl.multiple_of(i * (8 * group), 8) + 8 * begin
        for g in range(group):
            at = start + 8 * g
            here = rows8(at)

            def cell(c):
                v = self.settled(sv_in, c, at)
                q = (v - 2.0) + pltpu.reciprocal(v, approx=True)
                down, across = self.rate(1, c, here) * q, self.rate(0, c, here) * q
                sv_out[c, rows8(at + 8), :] = down
                return v - jnp.abs(down + across), across

            heads = [cell(h * R) for h in halves]
            tails = [cell(h * R + R - 1) for h in halves]
            east = [pltpu.roll(jnp.maximum(x[1], 0.0), 1, 1) for x in tails]
            west = [pltpu.roll(jnp.minimum(x[1], 0.0), 127, 1) for x in heads]
            for c in strips:
                kept, across = cell(c)
                kept = kept + pltpu.roll(jnp.maximum(across, 0.0), 1, 1)
                acc[c, here, :] = kept - pltpu.roll(jnp.minimum(across, 0.0), 127, 1)
            for h in halves:
                this = heads[h]
                value = this[0] + jnp.where(lane == 0, east[1 - h], east[h])
                for b in range(1, R):
                    after = cell(h * R + b) if b < R - 1 else tails[h]
                    acc[h * R + b - 1, here, :] = value - jnp.minimum(after[1], 0.0)
                    value = after[0] + jnp.maximum(this[1], 0.0)
                    this = after
                acc[h * R + R - 1, here, :] = value - jnp.where(lane == 127, west[1 - h], west[h])


def strip_map():
    lane = lanes()
    fine = jnp.where(lane >= 64, lane - 64, lane + (NY * R - 64))
    return fine % R, fine // R % 128


def gathered(left, right, column):
    b_of, y_of = column
    near_left = lanes() < 64
    out = None
    for b in range(R):
        found = picked(jnp.where(near_left, left[b], right[b]), y_of)
        out = found if b == 0 else jnp.where(b_of == b, found, out)
    return out


def assemble_kernel(stw_in, sta_in, r02_in, r13_in, from_a, from_b, stw, sta, r02, r13, sr, pay_c, pay_d):
    group, gx, gy = info_of()
    even_x, even_y = lax.rem(gx, 2) == 0, lax.rem(gy, 2) == 0
    lane = lanes()

    @pl.when(group == 1)
    def _():
        at_a = jnp.where(even_x, ROWS - HALO, 0)
        at_b = ROWS - HALO - at_a

        def one(c):
            def join(v, h, w, to):
                stw[c, to, :] = v
                r02[c, to, :] = h
                r13[c, to, :] = w

            for t in range(OWN // 8):
                here = rows8(HALO + 8 * t)
                join(stw_in[c, here, :], r02_in[c, here, :], r13_in[c, here, :], here)
            for src, at in ((from_a, at_a), (from_b, at_b)):
                for t in range(HALO // 8):
                    v, h, w = (src[rows8((k * MAIN + c) * HALO + 8 * t), :] for k in range(3))
                    join(jnp.where(v == 0.0, 1.0, v), h, w, rows8(at + 8 * t))

        loop(MAIN, one)
        column = strip_map()

        def strips(t):
            for k, src in enumerate((stw, r02, r13)):
                found = []
                for half in range(2):
                    here = rows8(8 * t + 128 * half)
                    got = gathered([src[b, here, :] for b in range(R)], [src[R + b, here, :] for b in range(R)], column)
                    found.append(got)
                    if k == 0:
                        stw[MAIN, here, :] = got
                    else:
                        sr[2 * k - 2, here, :] = got
                one, two = found
                turned = pltpu.roll(two, 64, 1)
                to_left = jnp.where(lane >= 64, one, turned)
                to_right = jnp.where(lane < 64, one, turned)
                pay_c[rows8(k * 128 + 8 * t), :] = jnp.where(even_y, to_right, to_left)
                pay_d[rows8(k * 128 + 8 * t), :] = jnp.where(even_y, to_left, to_right)

        loop(16, strips)

    @pl.when(group == 0)
    def _():
        sub = lax.broadcasted_iota(jnp.int32, (8, 128), 0)

        def one(c):
            for h in range(2):
                for t in range(2):
                    here = slice(24 * h + 8 * t, 24 * h + 8 * t + 8)
                    sta[c, here, :] = sta_in[c, here, :]
                a, b = (x[rows8((c * 2 + h) * 8), :] for x in (from_a, from_b))
                above, below = jnp.where(even_x, b, a), jnp.where(even_x, a, b)
                sta[c, 24 * h + 16 : 24 * h + 24, :] = jnp.where(sub >= 4, above, below)

        loop(CH, one)

        def pack(i):
            k, t = i // 3, lax.rem(i, 3)
            to_left = jnp.zeros((8, 128), F32)
            to_right = to_left
            for j in range(32):
                c = jnp.minimum(32 * k + j, CH - 1)
                here = (lane >= 4 * j) & (lane < 4 * j + 4)
                west = sta[c, rows8(8 * t), :]
                east = sta[c, rows8(24 + 8 * t), :]
                to_left = jnp.where(here, pltpu.roll(west, 4 * j, 1), to_left)
                to_right = jnp.where(here, pltpu.roll(east, (4 * j + 4) % 128, 1), to_right)
            pay_c[rows8(k * 24 + 8 * t), :] = jnp.where(even_y, to_right, to_left)
            pay_d[rows8(k * 24 + 8 * t), :] = jnp.where(even_y, to_left, to_right)

        loop(12, pack)


def atmosphere_column(load, flux, regime, put):
    mixing = jnp.where(regime == 2.0, 0.4, 0.05)
    efficiency = jnp.where(regime == 0.0, 0.3, jnp.where(regime == 1.0, 0.6, 0.9))
    heat, damp = load(0) + flux, load(LEVELS) + flux
    heat_below, damp_below = heat, damp
    total = jnp.zeros((8, 128), F32)
    for k in range(LEVELS):
        last = k == LEVELS - 1
        heat_above = heat if last else load(k + 1)
        damp_above = damp if last else load(LEVELS + k + 1)
        t = heat + mixing * (heat_above + heat_below - 2.0 * heat)
        m = damp + mixing * (damp_above + damp_below - 2.0 * damp)
        capacity = (0.8 * math.exp(-3.0 * k / LEVELS)) * jnp.exp(0.3 * t)
        formed = efficiency * jnp.maximum(m - capacity, 0.0)
        put(k, t + 0.5 * formed)
        put(LEVELS + k, m - formed)
        total = total + formed
        heat_below, damp_below, heat, damp = heat, damp, heat_above, damp_above
    return total * (2.0 / LEVELS)


BANDS = ((0, 16, HALO), (16, 4, HALO + OWN), (20, 4, HALO - 4 * R))


def strip_rain(h0, h1, side, t):
    lane = lanes()
    here = slice(8 * t, 8 * t + 8)
    y = (lane + 16) // R - 8
    left = jnp.where(
        y < 0, picked(side[here], jnp.clip(128 + y, 0, 127)), picked(h0[here], jnp.clip(y, 0, 127))
    )
    y = (lane + (NY * R - 64)) // R
    right = jnp.where(
        y < NY, picked(h1[here], jnp.clip(y - 128, 0, 127)), picked(side[here], jnp.clip(y - NY, 0, 127))
    )
    return left, right


def strip_flux(left, right):
    lane = lanes()
    out = []
    for x, start in (
        (left, jnp.where(lane < 64, 64 + R * lane, 64 + R * (lane - 128))),
        (right, jnp.where(lane < 64, 64 + R * lane, 64 + R * (lane - 128))),
    ):
        back = lambda v, n: pltpu.roll(v, 128 - n, 1)
        two = x + back(x, 1)
        four = two + back(two, 2)
        ten = four + back(four, 4) + back(two, 8)
        out.append(picked(ten, jnp.clip(start, 0, 127)))
    return out


def route_kernel(step, *refs):
    opening, closing = step == 0, step == STEPS - 1
    if opening:
        stw, sta, r02, r13, sr_in, done, from_c, from_d, new, new_a, sr, field = refs[:12]
        acc, sv0, sv1, rain, sums, side_a = refs[12:]
        fld = None
    elif closing:
        stw, sta, r02, r13, sr, fld, out, field = refs[:8]
        acc, sv0, sv1, rain, sums = refs[8:]
    else:
        stw, sta, r02, r13, sr, fld, new, new_a, field = refs[:9]
        acc, sv0, sv1, rain, sums = refs[9:]
    group, _, gy = info_of()
    even_y = lax.rem(gy, 2) == 0
    lane = lanes()
    ranges = RANGES[step]
    first = ranges[0][0]
    count = TILES - 2 * first

    @pl.when(group == 0)
    def _():
        if opening:

            def side(i):
                k, t = i // 3, lax.rem(i, 3)
                c, d = from_c[rows8(k * 24 + 8 * t), :], from_d[rows8(k * 24 + 8 * t), :]
                west, east = jnp.where(even_y, d, c), jnp.where(even_y, c, d)
                for j in range(32):
                    side_a[32 * k + j, rows8(8 * t), :] = jnp.where(
                        lane < 4,
                        pltpu.roll(east, (128 - 4 * j) % 128, 1),
                        jnp.where(lane >= 124, pltpu.roll(west, 124 - 4 * j, 1), 0.0),
                    )

            loop(12, side)

        if closing:

            def own(i):
                h, t = i // 2, lax.rem(i, 2)
                here = rows8(24 * h + 8 * t)
                for u in range(2):

                    @pl.when(h == u)
                    def _():
                        cols = slice(128 * u, 128 * u + 128)

                        def put(c, value):
                            out[c, rows8(8 * t), cols] = value

                        field[rows8(8 * t), cols] = atmosphere_column(
                            lambda c: sta[c, here, :], fld[here, :], sta[CH - 1, here, :], put
                        )

            loop(4, own)
        else:

            def block(load, here):
                def put(c, value):
                    new_a[c, here, :] = value

                regime = load(CH - 1)
                put(CH - 1, regime)
                flux = load(CH - 2) if opening else fld[here, :]
                field[here, :] = atmosphere_column(load, flux, regime, put)

            def inner(i):
                here = rows8(8 * i)
                block(lambda c: sta[c, here, :], here)

            def outer(t):
                block(lambda c: side_a[c, rows8(8 * t), :], rows8(48 + 8 * t))

            if opening:
                loop(6, inner)
                loop(3, outer)
            else:
                loop(9, inner)

    @pl.when(group == 1)
    def _():
        zero = jnp.zeros((8, 128), F32)
        if opening:

            def side(t):
                for half in range(2):
                    here = rows8(8 * t + 128 * half)
                    for k in range(3):
                        c, d = from_c[rows8(k * 128 + 8 * t), :], from_d[rows8(k * 128 + 8 * t), :]
                        west, east = jnp.where(even_y, d, c), jnp.where(even_y, c, d)
                        if half:
                            west, east = pltpu.roll(west, 64, 1), pltpu.roll(east, 64, 1)
                        if k == 0:
                            west = jnp.where(west == 0.0, 1.0, west)
                            east = jnp.where(east == 0.0, 1.0, east)
                        inner = sr_in[2 * k - 2, here, :] if k else stw[MAIN, here, :]
                        left = jnp.where(lane >= 64, inner, west)
                        right = jnp.where(lane < 64, inner, east)
                        if k == 0:
                            acc[MAIN, here, :] = left
                            acc[MAIN + 1, here, :] = right
                        else:
                            sr[2 * k - 2, here, :] = left
                            sr[2 * k - 1, here, :] = right

            loop(16, side)

        def of(main, k, c, here):
            return main[c, here, :] if c < MAIN else sr[2 * k + c - MAIN, here, :]

        if opening:

            def fill(t):
                for at in (8 * t, 8 * t + 8 * (TILES - EDGE_TILES)):
                    for c in range(MAIN):
                        acc[c, rows8(at), :] = stw[c, rows8(at), :]

        else:
            blocks = [fld[pl.ds(24 * i, 24), :] for i in range(3)]
            found = [strip_rain(*blocks, t) for t in range(3)]
            for at, n, fine in BANDS:
                if n == 16:
                    pieces = [b[:16] for b in blocks[:2]]
                    pieces += [jnp.concatenate([found[0][i], found[1][i]], 0) for i in range(2)]
                else:
                    cut = slice(at - 16, at - 12)
                    pieces = [b[at : at + 4] for b in blocks[:2]] + [found[2][i][cut] for i in range(2)]
                for i, piece in enumerate(pieces):
                    for a in range(R):
                        rain[i, pl.ds(fine + a, n, stride=R), :] = piece

            def fill(t):
                here = rows8(8 * (t + first))
                for c in range(NCH):
                    fall = rain[c // R if c < MAIN else c - MAIN + 2, here, :]
                    rate = jnp.abs(of(r02, 0, c, here) + of(r13, 1, c, here))
                    share = 0.275 + 1.75 * rate
                    acc[c, here, :] = stw[c, here, :] + share * fall

        loop(EDGE_TILES if opening else count, fill)

        def clear(t):
            for c in range(NCH):
                sv0[c, rows8(8 * (t + first)), :] = zero

        loop(count + 2, clear)
        for c in range(NCH):
            sv1[c, rows8(8 * first), :] = zero
            sv1[c, rows8(8 * (first + count + 1)), :] = zero

        flow = Flow(acc, lambda k, c, here: of((r02, r13)[k], k, c, here))
        strips = (MAIN, MAIN + 1)
        if opening:
            for c in range(MAIN):
                sv1[c, rows8(8 * (EDGE_TILES + 1)), :] = zero
                sv1[c, rows8(8 * (TILES - EDGE_TILES)), :] = zero

            def pair(_):
                for sv in ((sv0, sv1), (sv1, sv0)):
                    flow.substep(0, EDGE_TILES, *sv, range(2), (), 0)
                    flow.substep(TILES - EDGE_TILES, EDGE_TILES, *sv, range(2), (), 0)
                    loop(2, functools.partial(flow.substep, 0, TILES // 2, *sv, (), strips))

            loop(SUB // 2, pair)
        else:
            for begin, size, substeps in ranges:

                def pair(_):
                    times = (TILES - 2 * begin) // size
                    loop(times, functools.partial(flow.substep, begin, size, sv0, sv1, range(2), strips))
                    loop(times, functools.partial(flow.substep, begin, size, sv1, sv0, range(2), strips))

                loop(substeps // 2, pair)

        column = strip_map()
        start = HALO // 8 if closing else RANGES[step + 1][0][0]
        near_left = lane < 64

        row = lax.broadcasted_iota(jnp.int32, (8, 128), 0)

        def finish(at):
            here = rows8(at)
            v = [flow.settled(sv0, c, at) for c in range(NCH)]
            if opening:
                ready = (row + at >= HALO + SUB) & (row + at < ROWS - HALO - SUB)
                for c in range(MAIN):
                    v[c] = jnp.where(ready, done[c, here, :], v[c])
            for h in range(2):
                total = v[h * R]
                for b in range(1, R):
                    total = total + v[h * R + b]
                sums[h, here, :] = total - float(R)
            sums[2, here, :] = v[MAIN] - 1.0
            sums[3, here, :] = v[MAIN + 1] - 1.0
            if step % 2:
                strip = jnp.where(near_left, v[MAIN + 1], v[MAIN])
                if not closing:
                    inner = gathered(v[:R], v[R:MAIN], column)
                for b in range(R):
                    place = R * lane + b
                    index = jnp.where(near_left, place + 64, place - (128 * R - 64))
                    got = picked(strip, jnp.clip(index, 0, 127))
                    v[b] = jnp.where(place < 2 * SUB, got, v[b])
                    v[R + b] = jnp.where(index >= 64 - 2 * SUB, jnp.where(near_left, v[R + b], got), v[R + b])
                if not closing:
                    v[MAIN] = jnp.where(lane >= 64 + 2 * SUB, inner, v[MAIN])
                    v[MAIN + 1] = jnp.where(lane < 64 - 2 * SUB, inner, v[MAIN + 1])
            if closing:
                for c in range(MAIN):
                    acc[c, here, :] = 0.45 * (v[c] - 1.0)
            else:
                for c in range(NCH):
                    new[c, here, :] = 0.9 * v[c] + 0.1

        def two(t):
            for u in range(2):
                finish(16 * t + 8 * start + 8 * u)

        loop(TILES // 2 - start, two)
        scale = 0.1 / (2.0 * R * R)
        pooled = []
        for at, n, fine in BANDS[: 1 if closing else 3]:
            parts = []
            for i in range(4):
                total = sums[i, pl.ds(fine, n, stride=R), :]
                for a in range(1, R):
                    total = total + sums[i, pl.ds(fine + a, n, stride=R), :]
                parts.append(total * scale)
            pooled.append(parts)
        if not closing:
            for i in range(4):
                rain[i, 0:16, :] = pooled[0][i]
                rain[i, 16:20, :] = pooled[1][i]
                rain[i, 20:24, :] = pooled[2][i]
        for t in range(2 if closing else 3):
            rows = slice(8 * t, 8 * t + 8)
            if closing:
                h0, h1, west, east = (pooled[0][i][rows] for i in range(4))
            else:
                h0, h1, west, east = (rain[i, rows, :] for i in range(4))
            west, east = strip_flux(west, east)
            h0 = jnp.where(lane < 3, west, h0)
            h1 = jnp.where(lane >= 125, east, h1)
            if closing:
                field[rows, 0:128] = h0
                field[rows, 128:256] = h1
            else:
                field[rows, :] = h0
                field[24 + 8 * t : 32 + 8 * t, :] = h1
                field[48 + 8 * t : 56 + 8 * t, :] = jnp.where(lane < 64, east, west)
        if closing:

            def lay(a):
                for b in range(R):
                    for h in range(2):
                        out[a * R + b, :, 128 * h : 128 * h + 128] = acc[h * R + b, pl.ds(HALO + a, NX, stride=R), :]

            loop(R, lay)


def call(kernel, args, out, scratch=(), hbm=False, limit=20, flops=0):
    return pl.pallas_call(
        kernel,
        out_shape=[jax.ShapeDtypeStruct(s, F32) for s in out],
        in_specs=[pl.BlockSpec(memory_space=pltpu.HBM if hbm else pltpu.VMEM)] * len(args),
        out_specs=[pl.BlockSpec(memory_space=pltpu.VMEM)] * len(out),
        scratch_shapes=[pltpu.VMEM(x, F32) if isinstance(x, tuple) else x for x in scratch],
        compiler_params=pltpu.CompilerParams(vmem_limit_bytes=limit * MIB),
        cost_estimate=pl.CostEstimate(flops=flops, bytes_accessed=5 * MIB, transcendentals=0) if flops else None,
    )(*args)


def pairs(axis, odd):
    n = lax.axis_size(axis)
    found = [(i, i + 1) for i in range(odd, n - 1, 2)]
    return found + [(j, i) for i, j in found]


def on_device(domain_state, coupling_field, regime, land_class, flow_code):
    tile = (2 * LEVELS, NX, NY)
    full, water, air = (MAIN, ROWS, 128), (NCH, ROWS, 128), (CH, 72, 128)
    strips, rim, small = (4, ROWS, 128), (384, 128), (72, 128)
    flows, inner_flows = (NCH, SVR, 128), (MAIN, SVR, 128)
    args = (domain_state[0], coupling_field[0], regime, land_class, flow_code)
    held = (
        tile,
        (NX, NY),
        pltpu.VMEM((NX, NY), jnp.int32),
        pltpu.VMEM(tile, jnp.int32),
        pltpu.VMEM(tile, jnp.int32),
        pltpu.SemaphoreType.DMA((3, R)),
        pltpu.SemaphoreType.DMA((2,)),
    )
    pay_a, pay_b = call(
        prep_kernel, args, ((3 * EDGE, 128), (3 * EDGE, 128)), held + ((3 * MAIN, OWN, 128),), hbm=True, limit=56
    )
    from_a = lax.ppermute(pay_a, "gx", pairs("gx", 0))
    from_b = lax.ppermute(pay_b, "gx", pairs("gx", 1))
    stw, sta, r02, r13, done = call(
        early_kernel,
        args,
        (full, air, full, full, full),
        held + (full, inner_flows, inner_flows),
        hbm=True,
        limit=26,
        flops=200_000_000,
    )
    stw, sta, r02, r13, sr, pay_c, pay_d = call(
        assemble_kernel, (stw, sta, r02, r13, from_a, from_b), (water, air, full, full, strips, rim, rim)
    )
    from_c = lax.ppermute(pay_c, "gy", pairs("gy", 0))
    from_d = lax.ppermute(pay_d, "gy", pairs("gy", 1))
    scratch = (water, flows, flows, (4, ROWS, 128), (4, ROWS, 128))
    for step in range(STEPS):
        kernel = functools.partial(route_kernel, step)
        if step == 0:
            stw, sta, sr, field = call(
                kernel,
                (stw, sta, r02, r13, sr, done, from_c, from_d),
                (water, air, strips, small),
                scratch + ((128, 24, 128),),
            )
        elif step < STEPS - 1:
            stw, sta, field = call(
                kernel, (stw, sta, r02, r13, sr, field), (water, air, small), scratch
            )
        else:
            out, field = call(
                kernel, (stw, sta, r02, r13, sr, field), (tile, (NX, NY)), scratch
            )
        field = lax.ppermute(field, "group", [(0, 1), (1, 0)])
    return (out[None], field[None])


def solution(mesh):
    return jax.shard_map(
        on_device,
        mesh=mesh,
        in_specs=(
            P("group", None, "gx", "gy"),
            P("group", "gx", "gy"),
            P("gx", "gy"),
            P(None, "gx", "gy"),
            P(None, "gx", "gy"),
        ),
        out_specs=(P("group", None, "gx", "gy"), P("group", "gx", "gy")),
        check_vma=False,
    )
```

time: 190 us -> 143 us (0.75)
  Pallas kernels: 125 us -> 103 us
  waiting for transfers between devices: 46.2 us -> 28.6 us
  local copies, waits for them, and re-layouts: 8.54 us -> 0.63 us
    pallas_call x6 -> x7, Pallas kernels: 125 us -> 103 us  [call(): pl.pallas_call(kernel, out_shape=[jax.ShapeDtypeStruct(s, F32) for s in o...]
    ppermute x1, waiting for transfers between devices: 17.4 us -> 0.01 us  [on_device(): from_b = lax.ppermute(pay_b, 'gx', pairs('gx', 1))]
    unnamed x13 -> x11, local copies, waits for them, and re-layouts: 8.54 us -> 0.63 us
  transfers between devices with their start and end apart: 8 -> 8, of which waited for: 8 -> 6; matrix products, arithmetic and copies ran while one was open for 0% -> 0% of each run, Pallas kernels for 0% -> 14%
where the time goes in v2:
time: 143 us; the launch traced here: 142 us
  Pallas kernels  103 us (72%)
  waiting for transfers between devices  28.6 us (20%)
  starting transfers between devices  9.34 us (7%)
    pallas_call x7, Pallas kernels, call(): pl.pallas_call(kernel, out_shape=[jax.ShapeDtypeStruct(s, F32) for s in o...  103 us
    ppermute x4, waiting for transfers between devices, on_device(): field = lax.ppermute(field, 'group', [(0, 1), (1, 0)])  21.6 us
    ppermute x1, waiting for transfers between devices, on_device(): from_d = lax.ppermute(pay_d, 'gy', pairs('gy', 1))  6.08 us
    ppermute x1, starting transfers between devices, on_device(): from_d = lax.ppermute(pay_d, 'gy', pairs('gy', 1))  4.68 us
  transfers between devices with their start and end apart: 8, of which 6 were waited for; matrix products, arithmetic and copies ran while one was open for 0% of the time, Pallas kernels for 14%

profile of v2, /device:TPU:14, one launch (start us, length us, event | category | flops | bytes accessed | tf_op | source)
XLA Modules:
  0.0 142.5 jit_solution(13972865446392061279)
XLA Ops:
  0.6 0.0 copy-start.2
  0.6 0.0 copy-start.1
  0.7 0.0 copy-start.4
  0.7 0.0 copy-start.3
  0.7 0.0 copy-start
  0.7 6.2 %shard_map.69 = (f32[2880,128]{1,0:T(8,128)}, f32[2880,128]{1,0:T(8,128)}) custom-call(f32[100,16,256]{2,1,0:T(8,128)} %bitcast.4, f32[16,256]{1,0:T(8,128)} %bitcast.6, s32[16,256]{1,0:T(8,128)} %refs_2_.3, s32[100,16,256]{2,1,0:T(8,128)} %refs_3_.3, s32[100,16,256]{2,1,0:T(8,128)} %refs_4_.3), custom_call_target="tpu_custom_call" | custom-call | tf_op jit(solution)/shard_map/pallas_call | solution.py:663
  6.9 0.1 collective-permute-start
  7.0 2.4 %collective-permute-start.1 = (f32[2880,128]{1,0:T(8,128)}, f32[2880,128]{1,0:T(8,128)S(1)}, u32[]{:S(2)}, u32[]{:S(2)}) collective-permute-start(f32[2880,128]{1,0:T(8,128)} %get-tuple-element.33), channel_id=1, source_target_pairs={{8,16},{24,32},{40,48},{16,8},{32,24},{48,40},{9,17},{25,33},{41,4... | collective-permute-start | bytes 4423688 | tf_op jit(solution)/shard_map/ppermute | solution.py:699
  9.4 0.0 copy-done.2
  9.4 0.0 copy-done.1
  9.4 0.0 copy-done.4
  9.5 19.6 %shard_map.68 = (f32[20,256,128]{2,1,0:T(8,128)S(1)}, f32[102,72,128]{2,1,0:T(8,128)S(1)}, f32[20,256,128]{2,1,0:T(8,128)S(1)}, f32[20,256,128]{2,1,0:T(8,128)S(1)}, f32[20,256,128]{2,1,0:T(8,128)S(1)}) custom-call(f32[100,16,256]{2,1,0:T(8,128)S(1)} %bitcast.5, f32[16,256]{1,0:T(8,128)S(1)} %bitcast.7, s32[16,256]{1,0:T(8,128)S(1)} %copy-done.4, ...), custom_call_target="tpu_custom_call" | custom-call | flops 200000000 | bytes 5242880 | tf_op jit(solution)/shard_map/pallas_call | solution.py:663
  29.1 0.0 collective-permute-done.from_a
  29.1 0.0 collective-permute-done.1.from_b
  29.1 3.7 %shard_map.70 = (f32[22,256,128]{2,1,0:T(8,128)S(1)}, f32[102,72,128]{2,1,0:T(8,128)S(1)}, f32[20,256,128]{2,1,0:T(8,128)S(1)}, f32[20,256,128]{2,1,0:T(8,128)S(...) custom-call(f32[20,256,128]{2,1,0:T(8,128)S(1)} %get-tuple-element.28.stw_in, ...), custom_call_target="tpu_custom_call" | custom-call | tf_op jit(solution)/shard_map/pallas_call | solution.py:663
  32.8 2.0 %collective-permute-start.2 = (f32[384,128]{1,0:T(8,128)S(1)}, f32[384,128]{1,0:T(8,128)S(1)}, u32[]{:S(2)}, u32[]{:S(2)}) collective-permute-start(f32[384,128]{1,0:T(8,128)S(1)} %get-tuple-element.40), channel_id=1, source_target_pairs={{0,1},{2,3},{4,5},{6,7},{1,0},{3,2},{5,4},{7,6},{8,9},{10,11},{12,... | collective-permute-start | bytes 589832 | tf_op jit(solution)/shard_map/ppermute | solution.py:712
  34.7 4.7 %collective-permute-start.3 = (f32[384,128]{1,0:T(8,128)S(1)}, f32[384,128]{1,0:T(8,128)S(1)}, u32[]{:S(2)}, u32[]{:S(2)}) collective-permute-start(f32[384,128]{1,0:T(8,128)S(1)} %get-tuple-element.41), channel_id=1, source_target_pairs={{1,2},{3,4},{5,6},{2,1},{4,3},{6,5},{9,10},{11,12},{13,14},{10,9},... | collective-permute-start | bytes 589832 | tf_op jit(solution)/shard_map/ppermute | solution.py:713
  39.4 0.9 collective-permute-done.2.refs_6_
  40.3 6.1 %collective-permute-done.3.refs_7_ = f32[384,128]{1,0:T(8,128)S(1)} collective-permute-done((f32[384,128]{1,0:T(8,128)S(1)}, f32[384,128]{1,0:T(8,128)S(1)}, u32[]{:S(2)}, u32[]{:S(2)}) %collective-permute-start.3) | collective-permute-done | bytes 196640 | tf_op jit(solution)/shard_map/ppermute | solution.py:713
  46.4 16.4 %shard_map.71 = (f32[22,256,128]{2,1,0:T(8,128)S(1)}, f32[102,72,128]{2,1,0:T(8,128)S(1)}, f32[4,256,128]{2,1,0:T(8,128)S(1)}, f32[72,128]{1,0:T(8,128)S(1)}) custom-call(f32[22,256,128]{2,1,0:T(8,128)S(1)} %get-tuple-element.34.refs_0_, f32[102,72,128]{2,1,0:T(8,128)S(1)} %get-tuple-element.35.refs_1_, f32[20,256,128]{2,1,0:T(8,128)S(1)} %get-tuple-element.36.refs_2_, ...), custom_call_target="tpu_custom_call" | custom-call | tf_op jit(solution)/shard_map/pallas_call | solution.py:663
  62.8 0.1 collective-permute-start.4
  62.8 5.4 %collective-permute-done.4.refs_5_ = f32[72,128]{1,0:T(8,128)S(1)} collective-permute-done((f32[72,128]{1,0:T(8,128)S(1)}, f32[72,128]{1,0:T(8,128)S(1)}, u32[]{:S(2)}, u32[]{:S(2)}) %collective-permute-start.4) | collective-permute-done | bytes 36896 | tf_op jit(solution)/shard_map/ppermute | solution.py:732
  68.3 21.5 %shard_map.72 = (f32[22,256,128]{2,1,0:T(8,128)S(1)}, f32[102,72,128]{2,1,0:T(8,128)S(1)}, f32[72,128]{1,0:T(8,128)S(1)}) custom-call(f32[22,256,128]{2,1,0:T(8,128)S(1)} %get-tuple-element.42.refs_0_, f32[102,72,128]{2,1,0:T(8,128)S(1)} %get-tuple-element.43.refs_1_, f32[20,256,128]{2,1,0:T(8,128)S(1)} %get-tuple-element.36.refs_2_, ...), custom_call_target="tpu_custom_call" | custom-call | tf_op jit(solution)/shard_map/pallas_call | solution.py:663
  89.8 0.1 collective-permute-start.5
  89.9 5.4 %collective-permute-done.5.refs_5_ = f32[72,128]{1,0:T(8,128)S(1)} collective-permute-done((f32[72,128]{1,0:T(8,128)S(1)}, f32[72,128]{1,0:T(8,128)S(1)}, u32[]{:S(2)}, u32[]{:S(2)}) %collective-permute-start.5) | collective-permute-done | bytes 36896 | tf_op jit(solution)/shard_map/ppermute | solution.py:732
  95.3 17.8 %shard_map.73 = (f32[22,256,128]{2,1,0:T(8,128)S(1)}, f32[102,72,128]{2,1,0:T(8,128)S(1)}, f32[72,128]{1,0:T(8,128)S(1)}) custom-call(f32[22,256,128]{2,1,0:T(8,128)S(1)} %get-tuple-element.46.refs_0_, f32[102,72,128]{2,1,0:T(8,128)S(1)} %get-tuple-element.47.refs_1_, f32[20,256,128]{2,1,0:T(8,128)S(1)} %get-tuple-element.36.refs_2_, ...), custom_call_target="tpu_custom_call" | custom-call | tf_op jit(solution)/shard_map/pallas_call | solution.py:663
  113.1 0.1 collective-permute-start.6
  113.2 5.4 %collective-permute-done.6.refs_5_ = f32[72,128]{1,0:T(8,128)S(1)} collective-permute-done((f32[72,128]{1,0:T(8,128)S(1)}, f32[72,128]{1,0:T(8,128)S(1)}, u32[]{:S(2)}, u32[]{:S(2)}) %collective-permute-start.6) | collective-permute-done | bytes 36896 | tf_op jit(solution)/shard_map/ppermute | solution.py:732
  118.6 18.0 %shard_map.74 = (f32[100,16,256]{2,1,0:T(8,128)}, f32[16,256]{1,0:T(8,128)S(1)}) custom-call(f32[22,256,128]{2,1,0:T(8,128)S(1)} %get-tuple-element.49.refs_0_, f32[102,72,128]{2,1,0:T(8,128)S(1)} %get-tuple-element.50.refs_1_, f32[20,256,128]{2,1,0:T(8,128)S(1)} %get-tuple-element.36.refs_2_, f32[20,256,128]{2,1,0:T(8,128)S(1)} %get-tuple-element.37.refs_3_, ...), custom_call_target="tpu_custom_call" | custom-call | tf_op jit(solution)/shard_map/pallas_call | solution.py:663
  136.6 0.0 collective-permute-start.7
  136.6 5.2 %collective-permute-done.7 = f32[16,256]{1,0:T(8,128)S(1)} collective-permute-done((f32[16,256]{1,0:T(8,128)S(1)}, f32[16,256]{1,0:T(8,128)S(1)}, u32[]{:S(2)}, u32[]{:S(2)}) %collective-permute-start.7) | collective-permute-done | bytes 16416 | tf_op jit(solution)/shard_map/ppermute | solution.py:732
  141.9 0.6 copy.8
  (2 shorter events, 0.0 us)
Async XLA Ops:
  0.6 8.8 %copy-start.2 = (s32[100,16,256]{2,1,0:T(8,128)S(1)}, s32[100,16,256]{2,1,0:T(8,128)}, u32[]{:S(2)}) copy-start(s32[100,16,256]{2,1,0:T(8,128)} %refs_4_.3) | copy-start | bytes 4915204
  0.6 8.8 %copy-start.1 = (s32[100,16,256]{2,1,0:T(8,128)S(1)}, s32[100,16,256]{2,1,0:T(8,128)}, u32[]{:S(2)}) copy-start(s32[100,16,256]{2,1,0:T(8,128)} %refs_3_.3) | copy-start | bytes 4915204
  0.7 8.8 %copy-start.4 = (s32[16,256]{1,0:T(8,128)S(1)}, s32[16,256]{1,0:T(8,128)}, u32[]{:S(2)}) copy-start(s32[16,256]{1,0:T(8,128)} %refs_2_.3) | copy-start | bytes 49156
  0.7 8.8 %copy-start.3 = (f32[1,16,256]{2,1,0:T(8,128)S(1)}, f32[1,16,256]{2,1,0:T(8,128)}, u32[]{:S(2)}) copy-start(f32[1,16,256]{2,1,0:T(8,128)} %param.6) | copy-start | bytes 49156
  0.7 8.8 %copy-start = (f32[1,100,16,256]{3,2,1,0:T(8,128)S(1)}, f32[1,100,16,256]{3,2,1,0:T(8,128)}, u32[]{:S(2)}) copy-start(f32[1,100,16,256]{3,2,1,0:T(8,128)} %param.5) | copy-start | bytes 4915204
  6.9 22.2 %collective-permute-start = (f32[2880,128]{1,0:T(8,128)}, f32[2880,128]{1,0:T(8,128)S(1)}, u32[]{:S(2)}, u32[]{:S(2)}) collective-permute-start(f32[2880,128]{1,0:T(8,128)} %get-tuple-element.32), channel_id=1, source_target_pairs={{0,8},{16,24},{32,40},{48,56},{8,0},{24,16},{40,32},{56,48},{1,9},... | collective-permute-start | bytes 4423688 | tf_op jit(solution)/shard_map/ppermute | solution.py:698
  7.0 22.1 %collective-permute-start.1 = (f32[2880,128]{1,0:T(8,128)}, f32[2880,128]{1,0:T(8,128)S(1)}, u32[]{:S(2)}, u32[]{:S(2)}) collective-permute-start(f32[2880,128]{1,0:T(8,128)} %get-tuple-element.33), channel_id=1, source_target_pairs={{8,16},{24,32},{40,48},{16,8},{32,24},{48,40},{9,17},{25,33},{41,4... | collective-permute-start | bytes 4423688 | tf_op jit(solution)/shard_map/ppermute | solution.py:699
  32.8 7.6 %collective-permute-start.2 = (f32[384,128]{1,0:T(8,128)S(1)}, f32[384,128]{1,0:T(8,128)S(1)}, u32[]{:S(2)}, u32[]{:S(2)}) collective-permute-start(f32[384,128]{1,0:T(8,128)S(1)} %get-tuple-element.40), channel_id=1, source_target_pairs={{0,1},{2,3},{4,5},{6,7},{1,0},{3,2},{5,4},{7,6},{8,9},{10,11},{12,... | collective-permute-start | bytes 589832 | tf_op jit(solution)/shard_map/ppermute | solution.py:712
  34.7 11.7 %collective-permute-start.3 = (f32[384,128]{1,0:T(8,128)S(1)}, f32[384,128]{1,0:T(8,128)S(1)}, u32[]{:S(2)}, u32[]{:S(2)}) collective-permute-start(f32[384,128]{1,0:T(8,128)S(1)} %get-tuple-element.41), channel_id=1, source_target_pairs={{1,2},{3,4},{5,6},{2,1},{4,3},{6,5},{9,10},{11,12},{13,14},{10,9},... | collective-permute-start | bytes 589832 | tf_op jit(solution)/shard_map/ppermute | solution.py:713
  62.8 5.5 %collective-permute-start.4 = (f32[72,128]{1,0:T(8,128)S(1)}, f32[72,128]{1,0:T(8,128)S(1)}, u32[]{:S(2)}, u32[]{:S(2)}) collective-permute-start(f32[72,128]{1,0:T(8,128)S(1)} %get-tuple-element.45), channel_id=1, source_target_pairs={{0,64},{64,0},{1,65},{65,1},{2,66},{66,2},{3,67},{67,3},{4,68},{68... | collective-permute-start | bytes 110600 | tf_op jit(solution)/shard_map/ppermute | solution.py:732
  89.8 5.5 %collective-permute-start.5 = (f32[72,128]{1,0:T(8,128)S(1)}, f32[72,128]{1,0:T(8,128)S(1)}, u32[]{:S(2)}, u32[]{:S(2)}) collective-permute-start(f32[72,128]{1,0:T(8,128)S(1)} %get-tuple-element.48), channel_id=1, source_target_pairs={{0,64},{64,0},{1,65},{65,1},{2,66},{66,2},{3,67},{67,3},{4,68},{68... | collective-permute-start | bytes 110600 | tf_op jit(solution)/shard_map/ppermute | solution.py:732
  113.1 5.5 %collective-permute-start.6 = (f32[72,128]{1,0:T(8,128)S(1)}, f32[72,128]{1,0:T(8,128)S(1)}, u32[]{:S(2)}, u32[]{:S(2)}) collective-permute-start(f32[72,128]{1,0:T(8,128)S(1)} %get-tuple-element.51), channel_id=1, source_target_pairs={{0,64},{64,0},{1,65},{65,1},{2,66},{66,2},{3,67},{67,3},{4,68},{68... | collective-permute-start | bytes 110600 | tf_op jit(solution)/shard_map/ppermute | solution.py:732
  136.6 5.2 %collective-permute-start.7 = (f32[16,256]{1,0:T(8,128)S(1)}, f32[16,256]{1,0:T(8,128)S(1)}, u32[]{:S(2)}, u32[]{:S(2)}) collective-permute-start(f32[16,256]{1,0:T(8,128)S(1)} %get-tuple-element.53), channel_id=1, source_target_pairs={{0,64},{64,0},{1,65},{65,1},{2,66},{66,2},{3,67},{67,3},{4,68},{68... | collective-permute-start | bytes 49160 | tf_op jit(solution)/shard_map/ppermute | solution.py:732

commit v3 on v2

--- a/solution.py
+++ b/solution.py
@@ -71,10 +71,10 @@
 
     def start(self, kinds):
         for x in self.small:
-            x.start()
+            x.start(priority=1)
         for i in range(R):
             for k in range(kinds):
-                self.part(k, i).start()
+                self.part(k, i).start(priority=1)
         for x in self.small:
             x.wait()
 
@@ -121,8 +121,13 @@
 
 
 def prep_kernel(*refs):
-    pay_a, pay_b, own = refs[5], refs[6], refs[14]
+    pay_a, pay_b, own, sems = refs[14:]
     inputs = Inputs(refs[:5], refs[7:12], *refs[12:14])
+
+    def sent(i, start, n):
+        part = pl.ds(start, n)
+        return pltpu.make_async_copy((pay_a, pay_b)[i].at[part], refs[5 + i].at[part], sems.at[i, start // EDGE])
+
     group, gx, _ = info_of()
     even = lax.rem(gx, 2) == 0
 
@@ -139,7 +144,14 @@
                 pay_a[rows8(i * HALO + 8 * t), :] = own[i, rows8(low + 8 * t), :]
                 pay_b[rows8(i * HALO + 8 * t), :] = own[i, rows8(OWN - HALO - low + 8 * t), :]
 
-        loop(3 * MAIN, rim)
+        copies = []
+        for k in range(3):
+            loop(MAIN, lambda c: rim(k * MAIN + c))
+            copies += [sent(i, k * EDGE, EDGE) for i in range(2)]
+            for x in copies[-2:]:
+                x.start()
+        for x in copies:
+            x.wait()
 
     @pl.when(group == 0)
     def _():
@@ -153,6 +165,11 @@
                 pay_b[rows8((c * 2 + h) * 8), :] = value
 
         inputs.blocks(put)
+        copies = [sent(i, 0, CH * 16) for i in range(2)]
+        for x in copies:
+            x.start()
+        for x in copies:
+            x.wait()
 
 
 def early_kernel(*refs):
@@ -167,7 +184,7 @@
             (stw, r02, r13)[k][c, pl.ds(HALO + a, NX, stride=R), :] = value
 
         inputs.lay_out(put)
-        begin, size = HALO // 8, 10
+        begin = HALO // 8
 
         def fill(t):
             here = rows8(8 * (t + begin))
@@ -187,19 +204,22 @@
             sv1[c, rows8(HALO + OWN + 8), :] = zero
         flow = Flow(acc, lambda k, c, here: (r02, r13)[k][c, here, :])
 
-        def pair(_):
-            loop(OWN // (8 * size), functools.partial(flow.substep, begin, size, sv0, sv1, range(2), ()))
-            loop(OWN // (8 * size), functools.partial(flow.substep, begin, size, sv1, sv0, range(2), ()))
-
-        loop(SUB // 2, pair)
+        for trim, substeps in ((0, 8), (1, 4)):
+
+            def pair(_):
+                size = OWN // 16 - trim
+                for sv in ((sv0, sv1), (sv1, sv0)):
+                    loop(2, functools.partial(flow.substep, begin + trim, size, *sv, range(2), ()))
+
+            loop(substeps // 2, pair)
 
         def finish(t):
             for u in range(2):
-                at = 16 * t + HALO + 8 * u
+                at = 16 * t + HALO + 8 + 8 * u
                 for c in range(MAIN):
                     inner[c, rows8(at), :] = flow.settled(sv0, c, at)
 
-        loop(OWN // 16, finish)
+        loop(OWN // 16 - 1, finish)
 
     @pl.when(group == 0)
     def _():
@@ -400,14 +420,14 @@
 
 
 def route_kernel(step, *refs):
-    opening, closing = step == 0, step == STEPS - 1
+    opening, closing, merging = step == 0, step == STEPS - 1, step % 2 == 1
     if opening:
-        stw, sta, r02, r13, sr_in, done, from_c, from_d, new, new_a, sr, field = refs[:12]
+        stw, sta, r02, r13, sr_in, done, from_c, from_d, new, new_a, field, sr = refs[:12]
         acc, sv0, sv1, rain, sums, side_a = refs[12:]
         fld = None
-    elif closing:
-        stw, sta, r02, r13, sr, fld, out, field = refs[:8]
-        acc, sv0, sv1, rain, sums = refs[8:]
+    elif merging:
+        stw, sta, r02, r13, sr, fld, acc, sv0, new_a, field = refs[:10]
+        sv1, rain, sums = refs[10:]
     else:
         stw, sta, r02, r13, sr, fld, new, new_a, field = refs[:9]
         acc, sv0, sv1, rain, sums = refs[9:]
@@ -440,18 +460,16 @@
             def own(i):
                 h, t = i // 2, lax.rem(i, 2)
                 here = rows8(24 * h + 8 * t)
+
+                def put(c, value):
+                    new_a[c, here, :] = value
+
+                total = atmosphere_column(lambda c: sta[c, here, :], fld[here, :], sta[CH - 1, here, :], put)
                 for u in range(2):
 
                     @pl.when(h == u)
                     def _():
-                        cols = slice(128 * u, 128 * u + 128)
-
-                        def put(c, value):
-                            out[c, rows8(8 * t), cols] = value
-
-                        field[rows8(8 * t), cols] = atmosphere_column(
-                            lambda c: sta[c, here, :], fld[here, :], sta[CH - 1, here, :], put
-                        )
+                        field[rows8(8 * t), 128 * u : 128 * u + 128] = total
 
             loop(4, own)
         else:
@@ -556,13 +574,16 @@
                 sv1[c, rows8(8 * (EDGE_TILES + 1)), :] = zero
                 sv1[c, rows8(8 * (TILES - EDGE_TILES)), :] = zero
 
-            def pair(_):
-                for sv in ((sv0, sv1), (sv1, sv0)):
-                    flow.substep(0, EDGE_TILES, *sv, range(2), (), 0)
-                    flow.substep(TILES - EDGE_TILES, EDGE_TILES, *sv, range(2), (), 0)
-                    loop(2, functools.partial(flow.substep, 0, TILES // 2, *sv, (), strips))
-
-            loop(SUB // 2, pair)
+            for trim, substeps in ((0, 8), (1, 4)):
+
+                def pair(_):
+                    size = EDGE_TILES - 2 * trim
+                    for sv in ((sv0, sv1), (sv1, sv0)):
+                        flow.substep(trim, size, *sv, range(2), (), 0)
+                        flow.substep(TILES - trim - size, size, *sv, range(2), (), 0)
+                        loop(2, functools.partial(flow.substep, 0, TILES // 2, *sv, (), strips))
+
+                loop(substeps // 2, pair)
         else:
             for begin, size, substeps in ranges:
 
@@ -573,49 +594,29 @@
 
                 loop(substeps // 2, pair)
 
-        column = strip_map()
         start = HALO // 8 if closing else RANGES[step + 1][0][0]
-        near_left = lane < 64
-
-        row = lax.broadcasted_iota(jnp.int32, (8, 128), 0)
-
-        def finish(at):
+
+        def tally(at):
             here = rows8(at)
-            v = [flow.settled(sv0, c, at) for c in range(NCH)]
-            if opening:
-                ready = (row + at >= HALO + SUB) & (row + at < ROWS - HALO - SUB)
-                for c in range(MAIN):
-                    v[c] = jnp.where(ready, done[c, here, :], v[c])
             for h in range(2):
-                total = v[h * R]
-                for b in range(1, R):
-                    total = total + v[h * R + b]
+                total = None
+                for c in range(h * R, h * R + R):
+                    v = flow.settled(sv0, c, at)
+                    if opening:
+                        v = jnp.where(early_rows(at), done[c, here, :], v)
+                    if not merging:
+                        new[c, here, :] = 0.9 * v + 0.1
+                    total = v if total is None else total + v
                 sums[h, here, :] = total - float(R)
-            sums[2, here, :] = v[MAIN] - 1.0
-            sums[3, here, :] = v[MAIN + 1] - 1.0
-            if step % 2:
-                strip = jnp.where(near_left, v[MAIN + 1], v[MAIN])
-                if not closing:
-                    inner = gathered(v[:R], v[R:MAIN], column)
-                for b in range(R):
-                    place = R * lane + b
-                    index = jnp.where(near_left, place + 64, place - (128 * R - 64))
-                    got = picked(strip, jnp.clip(index, 0, 127))
-                    v[b] = jnp.where(place < 2 * SUB, got, v[b])
-                    v[R + b] = jnp.where(index >= 64 - 2 * SUB, jnp.where(near_left, v[R + b], got), v[R + b])
-                if not closing:
-                    v[MAIN] = jnp.where(lane >= 64 + 2 * SUB, inner, v[MAIN])
-                    v[MAIN + 1] = jnp.where(lane < 64 - 2 * SUB, inner, v[MAIN + 1])
-            if closing:
-                for c in range(MAIN):
-                    acc[c, here, :] = 0.45 * (v[c] - 1.0)
-            else:
-                for c in range(NCH):
-                    new[c, here, :] = 0.9 * v[c] + 0.1
+            for c in (MAIN, MAIN + 1):
+                v = flow.settled(sv0, c, at)
+                if not merging:
+                    new[c, here, :] = 0.9 * v + 0.1
+                sums[c - MAIN + 2, here, :] = v - 1.0
 
         def two(t):
             for u in range(2):
-                finish(16 * t + 8 * start + 8 * u)
+                tally(16 * t + 8 * start + 8 * u)
 
         loop(TILES // 2 - start, two)
         scale = 0.1 / (2.0 * R * R)
@@ -649,22 +650,83 @@
                 field[rows, :] = h0
                 field[24 + 8 * t : 32 + 8 * t, :] = h1
                 field[48 + 8 * t : 56 + 8 * t, :] = jnp.where(lane < 64, east, west)
+
+
+def early_rows(at):
+    row = lax.broadcasted_iota(jnp.int32, (8, 128), 0) + at
+    return (row >= HALO + SUB) & (row < ROWS - HALO - SUB)
+
+
+def settle_kernel(step, *refs):
+    closing = step == STEPS - 1
+    if closing:
+        acc, sv0, sta, out, last = refs
+    else:
+        acc, sv0, new = refs
+    group, _, _ = info_of()
+    lane = lanes()
+
+    @pl.when(group == 1)
+    def _():
+        flow = Flow(acc, None)
+        column = strip_map()
+        start = HALO // 8 if closing else RANGES[step + 1][0][0]
+        near_left = lane < 64
+
+        def finish(at):
+            here = rows8(at)
+            v = [flow.settled(sv0, c, at) for c in range(NCH)]
+            strip = jnp.where(near_left, v[MAIN + 1], v[MAIN])
+            if not closing:
+                inner = gathered(v[:R], v[R:MAIN], column)
+            for b in range(R):
+                place = R * lane + b
+                index = jnp.where(near_left, place + 64, place - (128 * R - 64))
+                got = picked(strip, jnp.clip(index, 0, 127))
+                v[b] = jnp.where(place < 2 * SUB, got, v[b])
+                v[R + b] = jnp.where(index >= 64 - 2 * SUB, jnp.where(near_left, v[R + b], got), v[R + b])
+            if not closing:
+                v[MAIN] = jnp.where(lane >= 64 + 2 * SUB, inner, v[MAIN])
+                v[MAIN + 1] = jnp.where(lane < 64 - 2 * SUB, inner, v[MAIN + 1])
+            if closing:
+                for c in range(MAIN):
+                    last[c, rows8(at - HALO), :] = 0.45 * (v[c] - 1.0)
+            else:
+                for c in range(NCH):
+                    new[c, here, :] = 0.9 * v[c] + 0.1
+
+        def two(t):
+            for u in range(2):
+                finish(16 * t + 8 * start + 8 * u)
+
+        loop(TILES // 2 - start, two)
         if closing:
 
             def lay(a):
                 for b in range(R):
                     for h in range(2):
-                        out[a * R + b, :, 128 * h : 128 * h + 128] = acc[h * R + b, pl.ds(HALO + a, NX, stride=R), :]
+                        out[a * R + b, :, 128 * h : 128 * h + 128] = last[h * R + b, pl.ds(a, NX, stride=R), :]
 
             loop(R, lay)
 
-
-def call(kernel, args, out, scratch=(), hbm=False, limit=20, flops=0):
+    if closing:
+
+        @pl.when(group == 0)
+        def _():
+            def copy(i):
+                for u in range(10):
+                    for h in range(2):
+                        out[i * 10 + u, :, 128 * h : 128 * h + 128] = sta[i * 10 + u, 24 * h : 24 * h + 16, :]
+
+            loop(R, copy)
+
+
+def call(kernel, args, out, scratch=(), hbm=False, out_hbm=False, limit=16, flops=0):
     return pl.pallas_call(
         kernel,
         out_shape=[jax.ShapeDtypeStruct(s, F32) for s in out],
         in_specs=[pl.BlockSpec(memory_space=pltpu.HBM if hbm else pltpu.VMEM)] * len(args),
-        out_specs=[pl.BlockSpec(memory_space=pltpu.VMEM)] * len(out),
+        out_specs=[pl.BlockSpec(memory_space=pltpu.HBM if out_hbm else pltpu.VMEM)] * len(out),
         scratch_shapes=[pltpu.VMEM(x, F32) if isinstance(x, tuple) else x for x in scratch],
         compiler_params=pltpu.CompilerParams(vmem_limit_bytes=limit * MIB),
         cost_estimate=pl.CostEstimate(flops=flops, bytes_accessed=5 * MIB, transcendentals=0) if flops else None,
@@ -692,8 +754,15 @@
         pltpu.SemaphoreType.DMA((3, R)),
         pltpu.SemaphoreType.DMA((2,)),
     )
+    edge = (3 * EDGE, 128)
     pay_a, pay_b = call(
-        prep_kernel, args, ((3 * EDGE, 128), (3 * EDGE, 128)), held + ((3 * MAIN, OWN, 128),), hbm=True, limit=56
+        prep_kernel,
+        args,
+        (edge, edge),
+        held + (edge, edge, (3 * MAIN, OWN, 128), pltpu.SemaphoreType.DMA((2, 3))),
+        hbm=True,
+        out_hbm=True,
+        limit=56,
     )
     from_a = lax.ppermute(pay_a, "gx", pairs("gx", 0))
     from_b = lax.ppermute(pay_b, "gx", pairs("gx", 1))
@@ -703,7 +772,7 @@
         (full, air, full, full, full),
         held + (full, inner_flows, inner_flows),
         hbm=True,
-        limit=26,
+        limit=17,
         flops=200_000_000,
     )
     stw, sta, r02, r13, sr, pay_c, pay_d = call(
@@ -711,25 +780,30 @@
     )
     from_c = lax.ppermute(pay_c, "gy", pairs("gy", 0))
     from_d = lax.ppermute(pay_d, "gy", pairs("gy", 1))
-    scratch = (water, flows, flows, (4, ROWS, 128), (4, ROWS, 128))
+    spare = (flows, (4, ROWS, 128), (4, ROWS, 128))
+    scratch = (water, flows) + spare
     for step in range(STEPS):
         kernel = functools.partial(route_kernel, step)
+        settle = functools.partial(settle_kernel, step)
         if step == 0:
-            stw, sta, sr, field = call(
+            stw, sta, field, sr = call(
                 kernel,
                 (stw, sta, r02, r13, sr, done, from_c, from_d),
-                (water, air, strips, small),
+                (water, air, small, strips),
                 scratch + ((128, 24, 128),),
             )
-        elif step < STEPS - 1:
-            stw, sta, field = call(
-                kernel, (stw, sta, r02, r13, sr, field), (water, air, small), scratch
-            )
+        elif step % 2 == 0:
+            stw, sta, field = call(kernel, (stw, sta, r02, r13, sr, field), (water, air, small), scratch)
         else:
-            out, field = call(
-                kernel, (stw, sta, r02, r13, sr, field), (tile, (NX, NY)), scratch
+            shape = (NX, NY) if step == STEPS - 1 else small
+            acc, sv, sta, field = call(
+                kernel, (stw, sta, r02, r13, sr, field), (water, flows, air, shape), spare
             )
         field = lax.ppermute(field, "group", [(0, 1), (1, 0)])
+        if step == STEPS - 1:
+            out = call(settle, (acc, sv, sta), (tile,), ((MAIN, OWN, 128),), flops=50_000_000)[0]
+        elif step % 2:
+            stw = call(settle, (acc, sv), (water,), flops=50_000_000)[0]
     return (out[None], field[None])
 
 

time: 143 us -> 140 us (0.979)
  waiting for transfers between devices: 28.6 us -> 23.7 us
  Pallas kernels: 103 us -> 106 us
    ppermute x4, waiting for transfers between devices: 21.6 us -> 16.7 us  [on_device(): field = lax.ppermute(field, 'group', [(0, 1), (1, 0)])]
    pallas_call x7 -> x9, Pallas kernels: 103 us -> 106 us  [call(): pl.pallas_call(kernel, out_shape=[jax.ShapeDtypeStruct(s, F32) for s in o...]
  transfers between devices with their start and end apart: 8 -> 8, of which waited for: 6 -> 6; matrix products, arithmetic and copies ran while one was open for 0% -> 0% of each run, Pallas kernels for 14% -> 18%
where the time goes in v3:
time: 140 us
  Pallas kernels  106 us (76%)
  waiting for transfers between devices  23.7 us (17%)
  starting transfers between devices  9.36 us (7%)
    pallas_call x9, Pallas kernels, call(): pl.pallas_call(kernel, out_shape=[jax.ShapeDtypeStruct(s, F32) for s in o...  106 us
    ppermute x4, waiting for transfers between devices, on_device(): field = lax.ppermute(field, 'group', [(0, 1), (1, 0)])  16.7 us
    ppermute x1, waiting for transfers between devices, on_device(): from_d = lax.ppermute(pay_d, 'gy', pairs('gy', 1))  6.08 us
    ppermute x1, starting transfers between devices, on_device(): from_d = lax.ppermute(pay_d, 'gy', pairs('gy', 1))  4.68 us
  transfers between devices with their start and end apart: 8, of which 6 were waited for; matrix products, arithmetic and copies ran while one was open for 0% of the time, Pallas kernels for 18%

profile of v3, /device:TPU:14, one launch (start us, length us, event | category | flops | bytes accessed | tf_op | source)
XLA Modules:
  0.0 140.1 jit_solution(11199197467616697887)
XLA Ops:
  0.6 0.0 copy-start.2
  0.6 0.0 copy-start.1
  0.7 0.0 copy-start.4
  0.7 0.0 copy-start.3
  0.7 0.0 copy-start
  0.7 5.8 %shard_map.69 = (f32[2880,128]{1,0:T(8,128)}, f32[2880,128]{1,0:T(8,128)}) custom-call(f32[100,16,256]{2,1,0:T(8,128)} %bitcast.4, f32[16,256]{1,0:T(8,128)} %bitcast.6, s32[16,256]{1,0:T(8,128)} %refs_2_.3, s32[100,16,256]{2,1,0:T(8,128)} %refs_3_.3, s32[100,16,256]{2,1,0:T(8,128)} %refs_4_.3), custom_call_target="tpu_custom_call" | custom-call | tf_op jit(solution)/shard_map/pallas_call | solution.py:725
  6.5 0.1 collective-permute-start
  6.6 2.4 %collective-permute-start.1 = (f32[2880,128]{1,0:T(8,128)}, f32[2880,128]{1,0:T(8,128)S(1)}, u32[]{:S(2)}, u32[]{:S(2)}) collective-permute-start(f32[2880,128]{1,0:T(8,128)} %get-tuple-element.36), channel_id=1, source_target_pairs={{8,16},{24,32},{40,48},{16,8},{32,24},{48,40},{9,17},{25,33},{41,4... | collective-permute-start | bytes 4423688 | tf_op jit(solution)/shard_map/ppermute | solution.py:768
  9.0 0.0 copy-done.2
  9.1 19.8 %shard_map.68 = (f32[20,256,128]{2,1,0:T(8,128)S(1)}, f32[102,72,128]{2,1,0:T(8,128)S(1)}, f32[20,256,128]{2,1,0:T(8,128)S(1)}, f32[20,256,128]{2,1,0:T(8,128)S(1)}, f32[20,256,128]{2,1,0:T(8,128)S(1)}) custom-call(f32[100,16,256]{2,1,0:T(8,128)S(1)} %bitcast.5, f32[16,256]{1,0:T(8,128)S(1)} %bitcast.7, s32[16,256]{1,0:T(8,128)S(1)} %copy-done.4, ...), custom_call_target="tpu_custom_call" | custom-call | flops 200000000 | bytes 5242880 | tf_op jit(solution)/shard_map/pallas_call | solution.py:725
  28.9 0.0 collective-permute-done.from_a
  28.9 0.0 collective-permute-done.1.from_b
  28.9 3.7 %shard_map.70 = (f32[22,256,128]{2,1,0:T(8,128)S(1)}, f32[102,72,128]{2,1,0:T(8,128)S(1)}, f32[20,256,128]{2,1,0:T(8,128)S(1)}, f32[20,256,128]{2,1,0:T(8,128)S(...) custom-call(f32[20,256,128]{2,1,0:T(8,128)S(1)} %get-tuple-element.31.stw_in, ...), custom_call_target="tpu_custom_call" | custom-call | tf_op jit(solution)/shard_map/pallas_call | solution.py:725
  32.6 2.0 %collective-permute-start.2 = (f32[384,128]{1,0:T(8,128)S(1)}, f32[384,128]{1,0:T(8,128)S(1)}, u32[]{:S(2)}, u32[]{:S(2)}) collective-permute-start(f32[384,128]{1,0:T(8,128)S(1)} %get-tuple-element.43), channel_id=1, source_target_pairs={{0,1},{2,3},{4,5},{6,7},{1,0},{3,2},{5,4},{7,6},{8,9},{10,11},{12,... | collective-permute-start | bytes 589832 | tf_op jit(solution)/shard_map/ppermute | solution.py:781
  34.5 4.7 %collective-permute-start.3 = (f32[384,128]{1,0:T(8,128)S(1)}, f32[384,128]{1,0:T(8,128)S(1)}, u32[]{:S(2)}, u32[]{:S(2)}) collective-permute-start(f32[384,128]{1,0:T(8,128)S(1)} %get-tuple-element.44), channel_id=1, source_target_pairs={{1,2},{3,4},{5,6},{2,1},{4,3},{6,5},{9,10},{11,12},{13,14},{10,9},... | collective-permute-start | bytes 589832 | tf_op jit(solution)/shard_map/ppermute | solution.py:782
  39.2 0.9 collective-permute-done.2.refs_6_
  40.1 6.1 %collective-permute-done.3.refs_7_ = f32[384,128]{1,0:T(8,128)S(1)} collective-permute-done((f32[384,128]{1,0:T(8,128)S(1)}, f32[384,128]{1,0:T(8,128)S(1)}, u32[]{:S(2)}, u32[]{:S(2)}) %collective-permute-start.3) | collective-permute-done | bytes 196640 | tf_op jit(solution)/shard_map/ppermute | solution.py:782
  46.2 15.7 %shard_map.71 = (f32[22,256,128]{2,1,0:T(8,128)S(1)}, f32[102,72,128]{2,1,0:T(8,128)S(1)}, f32[72,128]{1,0:T(8,128)S(1)}, f32[4,256,128]{2,1,0:T(8,128)S(1)}) custom-call(f32[22,256,128]{2,1,0:T(8,128)S(1)} %get-tuple-element.37.refs_0_, f32[102,72,128]{2,1,0:T(8,128)S(1)} %get-tuple-element.38.refs_1_, f32[20,256,128]{2,1,0:T(8,128)S(1)} %get-tuple-element.39.refs_2_, ...), custom_call_target="tpu_custom_call" | custom-call | tf_op jit(solution)/shard_map/pallas_call | solution.py:725
  61.9 0.1 collective-permute-start.4
  62.0 5.4 %collective-permute-done.4.refs_5_ = f32[72,128]{1,0:T(8,128)S(1)} collective-permute-done((f32[72,128]{1,0:T(8,128)S(1)}, f32[72,128]{1,0:T(8,128)S(1)}, u32[]{:S(2)}, u32[]{:S(2)}) %collective-permute-start.4) | collective-permute-done | bytes 36896 | tf_op jit(solution)/shard_map/ppermute | solution.py:802
  67.4 21.2 %shard_map.72 = (f32[22,256,128]{2,1,0:T(8,128)S(1)}, f32[22,272,128]{2,1,0:T(8,128)S(1)}, f32[102,72,128]{2,1,0:T(8,128)S(1)}, f32[72,128]{1,0:T(8,128)S(1)}) custom-call(f32[22,256,128]{2,1,0:T(8,128)S(1)} %get-tuple-element.45.refs_0_, f32[102,72,128]{2,1,0:T(8,128)S(1)} %get-tuple-element.46.refs_1_, f32[20,256,128]{2,1,0:T(8,128)S(1)} %get-tuple-element.39.refs_2_, ...), custom_call_target="tpu_custom_call" | custom-call | tf_op jit(solution)/shard_map/pallas_call | solution.py:725
  88.6 0.1 collective-permute-start.5
  88.7 2.2 %shard_map.73.refs_0_ = f32[22,256,128]{2,1,0:T(8,128)S(1)} custom-call(f32[22,256,128]{2,1,0:T(8,128)S(1)} %get-tuple-element.49.refs_0_, f32[22,272,128]{2,1,0:T(8,128)S(1)} %get-tuple-element.50.refs_1_), custom_call_target="tpu_custom_call" | custom-call | flops 50000000 | bytes 5242880 | tf_op jit(solution)/shard_map/pallas_call | solution.py:725
  90.9 3.2 %collective-permute-done.5.refs_5_ = f32[72,128]{1,0:T(8,128)S(1)} collective-permute-done((f32[72,128]{1,0:T(8,128)S(1)}, f32[72,128]{1,0:T(8,128)S(1)}, u32[]{:S(2)}, u32[]{:S(2)}) %collective-permute-start.5) | collective-permute-done | bytes 36896 | tf_op jit(solution)/shard_map/ppermute | solution.py:802
  94.1 17.9 %shard_map.74 = (f32[22,256,128]{2,1,0:T(8,128)S(1)}, f32[102,72,128]{2,1,0:T(8,128)S(1)}, f32[72,128]{1,0:T(8,128)S(1)}) custom-call(f32[22,256,128]{2,1,0:T(8,128)S(1)} %shard_map.73.refs_0_, f32[102,72,128]{2,1,0:T(8,128)S(1)} %get-tuple-element.51.refs_1_, f32[20,256,128]{2,1,0:T(8,128)S(1)} %get-tuple-element.39.refs_2_, ...), custom_call_target="tpu_custom_call" | custom-call | tf_op jit(solution)/shard_map/pallas_call | solution.py:725
  112.0 0.1 collective-permute-start.6
  112.1 5.4 %collective-permute-done.6.refs_5_ = f32[72,128]{1,0:T(8,128)S(1)} collective-permute-done((f32[72,128]{1,0:T(8,128)S(1)}, f32[72,128]{1,0:T(8,128)S(1)}, u32[]{:S(2)}, u32[]{:S(2)}) %collective-permute-start.6) | collective-permute-done | bytes 36896 | tf_op jit(solution)/shard_map/ppermute | solution.py:802
  117.5 16.7 %shard_map.75 = (f32[22,256,128]{2,1,0:T(8,128)S(1)}, f32[22,272,128]{2,1,0:T(8,128)S(1)}, f32[102,72,128]{2,1,0:T(8,128)S(1)}, f32[16,256]{1,0:T(8,128)S(1)}) custom-call(f32[22,256,128]{2,1,0:T(8,128)S(1)} %get-tuple-element.53.refs_0_, f32[102,72,128]{2,1,0:T(8,128)S(1)} %get-tuple-element.54.refs_1_, f32[20,256,128]{2,1,0:T(8,128)S(1)} %get-tuple-element.39.refs_2_, ...), custom_call_target="tpu_custom_call" | custom-call | tf_op jit(solution)/shard_map/pallas_call | solution.py:725
  134.2 0.0 collective-permute-start.7
  134.3 2.6 %shard_map.76 = f32[100,16,256]{2,1,0:T(8,128)} custom-call(f32[22,256,128]{2,1,0:T(8,128)S(1)} %get-tuple-element.56.refs_0_, f32[22,272,128]{2,1,0:T(8,128)S(1)} %get-tuple-element.57.refs_1_, f32[102,72,128]{2,1,0:T(8,128)S(1)} %get-tuple-element.58.refs_2_), custom_call_target="tpu_custom_call" | custom-call | flops 50000000 | bytes 5242880 | tf_op jit(solution)/shard_map/pallas_call | solution.py:725
  136.9 2.6 %collective-permute-done.7 = f32[16,256]{1,0:T(8,128)S(1)} collective-permute-done((f32[16,256]{1,0:T(8,128)S(1)}, f32[16,256]{1,0:T(8,128)S(1)}, u32[]{:S(2)}, u32[]{:S(2)}) %collective-permute-start.7) | collective-permute-done | bytes 16416 | tf_op jit(solution)/shard_map/ppermute | solution.py:802
  139.5 0.6 copy.8
  (4 shorter events, 0.0 us)
Async XLA Ops:
  0.6 8.4 %copy-start.2 = (s32[100,16,256]{2,1,0:T(8,128)S(1)}, s32[100,16,256]{2,1,0:T(8,128)}, u32[]{:S(2)}) copy-start(s32[100,16,256]{2,1,0:T(8,128)} %refs_4_.3) | copy-start | bytes 4915204
  0.6 8.4 %copy-start.1 = (s32[100,16,256]{2,1,0:T(8,128)S(1)}, s32[100,16,256]{2,1,0:T(8,128)}, u32[]{:S(2)}) copy-start(s32[100,16,256]{2,1,0:T(8,128)} %refs_3_.3) | copy-start | bytes 4915204
  0.7 8.4 %copy-start.4 = (s32[16,256]{1,0:T(8,128)S(1)}, s32[16,256]{1,0:T(8,128)}, u32[]{:S(2)}) copy-start(s32[16,256]{1,0:T(8,128)} %refs_2_.3) | copy-start | bytes 49156
  0.7 8.4 %copy-start.3 = (f32[1,16,256]{2,1,0:T(8,128)S(1)}, f32[1,16,256]{2,1,0:T(8,128)}, u32[]{:S(2)}) copy-start(f32[1,16,256]{2,1,0:T(8,128)} %param.6) | copy-start | bytes 49156
  0.7 8.4 %copy-start = (f32[1,100,16,256]{3,2,1,0:T(8,128)S(1)}, f32[1,100,16,256]{3,2,1,0:T(8,128)}, u32[]{:S(2)}) copy-start(f32[1,100,16,256]{3,2,1,0:T(8,128)} %param.5) | copy-start | bytes 4915204
  6.5 22.4 %collective-permute-start = (f32[2880,128]{1,0:T(8,128)}, f32[2880,128]{1,0:T(8,128)S(1)}, u32[]{:S(2)}, u32[]{:S(2)}) collective-permute-start(f32[2880,128]{1,0:T(8,128)} %get-tuple-element.35), channel_id=1, source_target_pairs={{0,8},{16,24},{32,40},{48,56},{8,0},{24,16},{40,32},{56,48},{1,9},... | collective-permute-start | bytes 4423688 | tf_op jit(solution)/shard_map/ppermute | solution.py:767
  6.6 22.3 %collective-permute-start.1 = (f32[2880,128]{1,0:T(8,128)}, f32[2880,128]{1,0:T(8,128)S(1)}, u32[]{:S(2)}, u32[]{:S(2)}) collective-permute-start(f32[2880,128]{1,0:T(8,128)} %get-tuple-element.36), channel_id=1, source_target_pairs={{8,16},{24,32},{40,48},{16,8},{32,24},{48,40},{9,17},{25,33},{41,4... | collective-permute-start | bytes 4423688 | tf_op jit(solution)/shard_map/ppermute | solution.py:768
  32.6 7.6 %collective-permute-start.2 = (f32[384,128]{1,0:T(8,128)S(1)}, f32[384,128]{1,0:T(8,128)S(1)}, u32[]{:S(2)}, u32[]{:S(2)}) collective-permute-start(f32[384,128]{1,0:T(8,128)S(1)} %get-tuple-element.43), channel_id=1, source_target_pairs={{0,1},{2,3},{4,5},{6,7},{1,0},{3,2},{5,4},{7,6},{8,9},{10,11},{12,... | collective-permute-start | bytes 589832 | tf_op jit(solution)/shard_map/ppermute | solution.py:781
  34.5 11.7 %collective-permute-start.3 = (f32[384,128]{1,0:T(8,128)S(1)}, f32[384,128]{1,0:T(8,128)S(1)}, u32[]{:S(2)}, u32[]{:S(2)}) collective-permute-start(f32[384,128]{1,0:T(8,128)S(1)} %get-tuple-element.44), channel_id=1, source_target_pairs={{1,2},{3,4},{5,6},{2,1},{4,3},{6,5},{9,10},{11,12},{13,14},{10,9},... | collective-permute-start | bytes 589832 | tf_op jit(solution)/shard_map/ppermute | solution.py:782
  61.9 5.5 %collective-permute-start.4 = (f32[72,128]{1,0:T(8,128)S(1)}, f32[72,128]{1,0:T(8,128)S(1)}, u32[]{:S(2)}, u32[]{:S(2)}) collective-permute-start(f32[72,128]{1,0:T(8,128)S(1)} %get-tuple-element.48), channel_id=1, source_target_pairs={{0,64},{64,0},{1,65},{65,1},{2,66},{66,2},{3,67},{67,3},{4,68},{68... | collective-permute-start | bytes 110600 | tf_op jit(solution)/shard_map/ppermute | solution.py:802
  88.6 5.5 %collective-permute-start.5 = (f32[72,128]{1,0:T(8,128)S(1)}, f32[72,128]{1,0:T(8,128)S(1)}, u32[]{:S(2)}, u32[]{:S(2)}) collective-permute-start(f32[72,128]{1,0:T(8,128)S(1)} %get-tuple-element.52), channel_id=1, source_target_pairs={{0,64},{64,0},{1,65},{65,1},{2,66},{66,2},{3,67},{67,3},{4,68},{68... | collective-permute-start | bytes 110600 | tf_op jit(solution)/shard_map/ppermute | solution.py:802
  112.0 5.5 %collective-permute-start.6 = (f32[72,128]{1,0:T(8,128)S(1)}, f32[72,128]{1,0:T(8,128)S(1)}, u32[]{:S(2)}, u32[]{:S(2)}) collective-permute-start(f32[72,128]{1,0:T(8,128)S(1)} %get-tuple-element.55), channel_id=1, source_target_pairs={{0,64},{64,0},{1,65},{65,1},{2,66},{66,2},{3,67},{67,3},{4,68},{68... | collective-permute-start | bytes 110600 | tf_op jit(solution)/shard_map/ppermute | solution.py:802
  134.2 5.3 %collective-permute-start.7 = (f32[16,256]{1,0:T(8,128)S(1)}, f32[16,256]{1,0:T(8,128)S(1)}, u32[]{:S(2)}, u32[]{:S(2)}) collective-permute-start(f32[16,256]{1,0:T(8,128)S(1)} %get-tuple-element.59), channel_id=1, source_target_pairs={{0,64},{64,0},{1,65},{65,1},{2,66},{66,2},{3,67},{67,3},{4,68},{68... | collective-permute-start | bytes 49160 | tf_op jit(solution)/shard_map/ppermute | solution.py:802

commit v4 on v3

--- a/solution.py
+++ b/solution.py
@@ -549,21 +549,28 @@
                         rain[i, pl.ds(fine + a, n, stride=R), :] = piece
 
             def fill(t):
-                here = rows8(8 * (t + first))
-                for c in range(NCH):
-                    fall = rain[c // R if c < MAIN else c - MAIN + 2, here, :]
-                    rate = jnp.abs(of(r02, 0, c, here) + of(r13, 1, c, here))
-                    share = 0.275 + 1.75 * rate
-                    acc[c, here, :] = stw[c, here, :] + share * fall
-
-        loop(EDGE_TILES if opening else count, fill)
+                for u in range(2):
+                    at = 16 * t + 8 * first + 8 * u
+                    here = rows8(at)
+                    for c in range(NCH):
+                        fall = rain[c // R if c < MAIN else c - MAIN + 2, here, :]
+                        rate = jnp.abs(of(r02, 0, c, here) + of(r13, 1, c, here))
+                        share = 0.275 + 1.75 * rate
+                        acc[c, here, :] = stw[c, here, :] + share * fall
+                        sv0[c, rows8(at + 8), :] = zero
+
+        loop(EDGE_TILES if opening else count // 2, fill)
 
         def clear(t):
             for c in range(NCH):
                 sv0[c, rows8(8 * (t + first)), :] = zero
 
-        loop(count + 2, clear)
+        if opening:
+            loop(count + 2, clear)
         for c in range(NCH):
+            if not opening:
+                sv0[c, rows8(8 * first), :] = zero
+                sv0[c, rows8(8 * (first + count + 1)), :] = zero
             sv1[c, rows8(8 * first), :] = zero
             sv1[c, rows8(8 * (first + count + 1)), :] = zero
 

time: 140 us -> 139 us (level)
  no operation moved by 1% of the time
where the time goes in v4:
time: 139 us
  Pallas kernels  105 us (76%)
  waiting for transfers between devices  23.7 us (17%)
  starting transfers between devices  9.36 us (7%)
    pallas_call x9, Pallas kernels, call(): pl.pallas_call(kernel, out_shape=[jax.ShapeDtypeStruct(s, F32) for s in o...  105 us
    ppermute x4, waiting for transfers between devices, on_device(): field = lax.ppermute(field, 'group', [(0, 1), (1, 0)])  16.7 us
    ppermute x1, waiting for transfers between devices, on_device(): from_d = lax.ppermute(pay_d, 'gy', pairs('gy', 1))  6.08 us
    ppermute x1, starting transfers between devices, on_device(): from_d = lax.ppermute(pay_d, 'gy', pairs('gy', 1))  4.68 us
  transfers between devices with their start and end apart: 8, of which 6 were waited for; matrix products, arithmetic and copies ran while one was open for 0% of the time, Pallas kernels for 18%

profile of v4, /device:TPU:14, one launch (start us, length us, event | category | flops | bytes accessed | tf_op | source)
XLA Modules:
  0.0 139.0 jit_solution(17593447806710836170)
XLA Ops:
  0.6 0.0 copy-start.2
  0.6 0.0 copy-start.1
  0.7 0.0 copy-start.4
  0.7 0.0 copy-start.3
  0.7 0.0 copy-start
  0.7 5.8 %shard_map.69 = (f32[2880,128]{1,0:T(8,128)}, f32[2880,128]{1,0:T(8,128)}) custom-call(f32[100,16,256]{2,1,0:T(8,128)} %bitcast.4, f32[16,256]{1,0:T(8,128)} %bitcast.6, s32[16,256]{1,0:T(8,128)} %refs_2_.3, s32[100,16,256]{2,1,0:T(8,128)} %refs_3_.3, s32[100,16,256]{2,1,0:T(8,128)} %refs_4_.3), custom_call_target="tpu_custom_call" | custom-call | tf_op jit(solution)/shard_map/pallas_call | solution.py:732
  6.5 0.1 collective-permute-start
  6.6 2.4 %collective-permute-start.1 = (f32[2880,128]{1,0:T(8,128)}, f32[2880,128]{1,0:T(8,128)S(1)}, u32[]{:S(2)}, u32[]{:S(2)}) collective-permute-start(f32[2880,128]{1,0:T(8,128)} %get-tuple-element.36), channel_id=1, source_target_pairs={{8,16},{24,32},{40,48},{16,8},{32,24},{48,40},{9,17},{25,33},{41,4... | collective-permute-start | bytes 4423688 | tf_op jit(solution)/shard_map/ppermute | solution.py:775
  9.0 0.0 copy-done.2
  9.1 19.8 %shard_map.68 = (f32[20,256,128]{2,1,0:T(8,128)S(1)}, f32[102,72,128]{2,1,0:T(8,128)S(1)}, f32[20,256,128]{2,1,0:T(8,128)S(1)}, f32[20,256,128]{2,1,0:T(8,128)S(1)}, f32[20,256,128]{2,1,0:T(8,128)S(1)}) custom-call(f32[100,16,256]{2,1,0:T(8,128)S(1)} %bitcast.5, f32[16,256]{1,0:T(8,128)S(1)} %bitcast.7, s32[16,256]{1,0:T(8,128)S(1)} %copy-done.4, ...), custom_call_target="tpu_custom_call" | custom-call | flops 200000000 | bytes 5242880 | tf_op jit(solution)/shard_map/pallas_call | solution.py:732
  28.9 0.0 collective-permute-done.from_a
  28.9 0.0 collective-permute-done.1.from_b
  28.9 3.7 %shard_map.70 = (f32[22,256,128]{2,1,0:T(8,128)S(1)}, f32[102,72,128]{2,1,0:T(8,128)S(1)}, f32[20,256,128]{2,1,0:T(8,128)S(1)}, f32[20,256,128]{2,1,0:T(8,128)S(...) custom-call(f32[20,256,128]{2,1,0:T(8,128)S(1)} %get-tuple-element.31.stw_in, ...), custom_call_target="tpu_custom_call" | custom-call | tf_op jit(solution)/shard_map/pallas_call | solution.py:732
  32.6 2.0 %collective-permute-start.2 = (f32[384,128]{1,0:T(8,128)S(1)}, f32[384,128]{1,0:T(8,128)S(1)}, u32[]{:S(2)}, u32[]{:S(2)}) collective-permute-start(f32[384,128]{1,0:T(8,128)S(1)} %get-tuple-element.43), channel_id=1, source_target_pairs={{0,1},{2,3},{4,5},{6,7},{1,0},{3,2},{5,4},{7,6},{8,9},{10,11},{12,... | collective-permute-start | bytes 589832 | tf_op jit(solution)/shard_map/ppermute | solution.py:788
  34.5 4.7 %collective-permute-start.3 = (f32[384,128]{1,0:T(8,128)S(1)}, f32[384,128]{1,0:T(8,128)S(1)}, u32[]{:S(2)}, u32[]{:S(2)}) collective-permute-start(f32[384,128]{1,0:T(8,128)S(1)} %get-tuple-element.44), channel_id=1, source_target_pairs={{1,2},{3,4},{5,6},{2,1},{4,3},{6,5},{9,10},{11,12},{13,14},{10,9},... | collective-permute-start | bytes 589832 | tf_op jit(solution)/shard_map/ppermute | solution.py:789
  39.2 0.9 collective-permute-done.2.refs_6_
  40.1 6.1 %collective-permute-done.3.refs_7_ = f32[384,128]{1,0:T(8,128)S(1)} collective-permute-done((f32[384,128]{1,0:T(8,128)S(1)}, f32[384,128]{1,0:T(8,128)S(1)}, u32[]{:S(2)}, u32[]{:S(2)}) %collective-permute-start.3) | collective-permute-done | bytes 196640 | tf_op jit(solution)/shard_map/ppermute | solution.py:789
  46.2 15.7 %shard_map.71 = (f32[22,256,128]{2,1,0:T(8,128)S(1)}, f32[102,72,128]{2,1,0:T(8,128)S(1)}, f32[72,128]{1,0:T(8,128)S(1)}, f32[4,256,128]{2,1,0:T(8,128)S(1)}) custom-call(f32[22,256,128]{2,1,0:T(8,128)S(1)} %get-tuple-element.37.refs_0_, f32[102,72,128]{2,1,0:T(8,128)S(1)} %get-tuple-element.38.refs_1_, f32[20,256,128]{2,1,0:T(8,128)S(1)} %get-tuple-element.39.refs_2_, ...), custom_call_target="tpu_custom_call" | custom-call | tf_op jit(solution)/shard_map/pallas_call | solution.py:732
  61.9 0.1 collective-permute-start.4
  62.0 5.4 %collective-permute-done.4.refs_5_ = f32[72,128]{1,0:T(8,128)S(1)} collective-permute-done((f32[72,128]{1,0:T(8,128)S(1)}, f32[72,128]{1,0:T(8,128)S(1)}, u32[]{:S(2)}, u32[]{:S(2)}) %collective-permute-start.4) | collective-permute-done | bytes 36896 | tf_op jit(solution)/shard_map/ppermute | solution.py:809
  67.4 20.7 %shard_map.72 = (f32[22,256,128]{2,1,0:T(8,128)S(1)}, f32[22,272,128]{2,1,0:T(8,128)S(1)}, f32[102,72,128]{2,1,0:T(8,128)S(1)}, f32[72,128]{1,0:T(8,128)S(1)}) custom-call(f32[22,256,128]{2,1,0:T(8,128)S(1)} %get-tuple-element.45.refs_0_, f32[102,72,128]{2,1,0:T(8,128)S(1)} %get-tuple-element.46.refs_1_, f32[20,256,128]{2,1,0:T(8,128)S(1)} %get-tuple-element.39.refs_2_, ...), custom_call_target="tpu_custom_call" | custom-call | tf_op jit(solution)/shard_map/pallas_call | solution.py:732
  88.2 0.1 collective-permute-start.5
  88.2 2.2 %shard_map.73.refs_0_ = f32[22,256,128]{2,1,0:T(8,128)S(1)} custom-call(f32[22,256,128]{2,1,0:T(8,128)S(1)} %get-tuple-element.49.refs_0_, f32[22,272,128]{2,1,0:T(8,128)S(1)} %get-tuple-element.50.refs_1_), custom_call_target="tpu_custom_call" | custom-call | flops 50000000 | bytes 5242880 | tf_op jit(solution)/shard_map/pallas_call | solution.py:732
  90.5 3.2 %collective-permute-done.5.refs_5_ = f32[72,128]{1,0:T(8,128)S(1)} collective-permute-done((f32[72,128]{1,0:T(8,128)S(1)}, f32[72,128]{1,0:T(8,128)S(1)}, u32[]{:S(2)}, u32[]{:S(2)}) %collective-permute-start.5) | collective-permute-done | bytes 36896 | tf_op jit(solution)/shard_map/ppermute | solution.py:809
  93.7 17.5 %shard_map.74 = (f32[22,256,128]{2,1,0:T(8,128)S(1)}, f32[102,72,128]{2,1,0:T(8,128)S(1)}, f32[72,128]{1,0:T(8,128)S(1)}) custom-call(f32[22,256,128]{2,1,0:T(8,128)S(1)} %shard_map.73.refs_0_, f32[102,72,128]{2,1,0:T(8,128)S(1)} %get-tuple-element.51.refs_1_, f32[20,256,128]{2,1,0:T(8,128)S(1)} %get-tuple-element.39.refs_2_, ...), custom_call_target="tpu_custom_call" | custom-call | tf_op jit(solution)/shard_map/pallas_call | solution.py:732
  111.2 0.1 collective-permute-start.6
  111.3 5.4 %collective-permute-done.6.refs_5_ = f32[72,128]{1,0:T(8,128)S(1)} collective-permute-done((f32[72,128]{1,0:T(8,128)S(1)}, f32[72,128]{1,0:T(8,128)S(1)}, u32[]{:S(2)}, u32[]{:S(2)}) %collective-permute-start.6) | collective-permute-done | bytes 36896 | tf_op jit(solution)/shard_map/ppermute | solution.py:809
  116.7 16.4 %shard_map.75 = (f32[22,256,128]{2,1,0:T(8,128)S(1)}, f32[22,272,128]{2,1,0:T(8,128)S(1)}, f32[102,72,128]{2,1,0:T(8,128)S(1)}, f32[16,256]{1,0:T(8,128)S(1)}) custom-call(f32[22,256,128]{2,1,0:T(8,128)S(1)} %get-tuple-element.53.refs_0_, f32[102,72,128]{2,1,0:T(8,128)S(1)} %get-tuple-element.54.refs_1_, f32[20,256,128]{2,1,0:T(8,128)S(1)} %get-tuple-element.39.refs_2_, ...), custom_call_target="tpu_custom_call" | custom-call | tf_op jit(solution)/shard_map/pallas_call | solution.py:732
  133.1 0.0 collective-permute-start.7
  133.2 2.6 %shard_map.76 = f32[100,16,256]{2,1,0:T(8,128)} custom-call(f32[22,256,128]{2,1,0:T(8,128)S(1)} %get-tuple-element.56.refs_0_, f32[22,272,128]{2,1,0:T(8,128)S(1)} %get-tuple-element.57.refs_1_, f32[102,72,128]{2,1,0:T(8,128)S(1)} %get-tuple-element.58.refs_2_), custom_call_target="tpu_custom_call" | custom-call | flops 50000000 | bytes 5242880 | tf_op jit(solution)/shard_map/pallas_call | solution.py:732
  135.8 2.6 %collective-permute-done.7 = f32[16,256]{1,0:T(8,128)S(1)} collective-permute-done((f32[16,256]{1,0:T(8,128)S(1)}, f32[16,256]{1,0:T(8,128)S(1)}, u32[]{:S(2)}, u32[]{:S(2)}) %collective-permute-start.7) | collective-permute-done | bytes 16416 | tf_op jit(solution)/shard_map/ppermute | solution.py:809
  138.4 0.6 copy.8
  (4 shorter events, 0.0 us)
Async XLA Ops:
  0.6 8.4 %copy-start.2 = (s32[100,16,256]{2,1,0:T(8,128)S(1)}, s32[100,16,256]{2,1,0:T(8,128)}, u32[]{:S(2)}) copy-start(s32[100,16,256]{2,1,0:T(8,128)} %refs_4_.3) | copy-start | bytes 4915204
  0.6 8.4 %copy-start.1 = (s32[100,16,256]{2,1,0:T(8,128)S(1)}, s32[100,16,256]{2,1,0:T(8,128)}, u32[]{:S(2)}) copy-start(s32[100,16,256]{2,1,0:T(8,128)} %refs_3_.3) | copy-start | bytes 4915204
  0.7 8.4 %copy-start.4 = (s32[16,256]{1,0:T(8,128)S(1)}, s32[16,256]{1,0:T(8,128)}, u32[]{:S(2)}) copy-start(s32[16,256]{1,0:T(8,128)} %refs_2_.3) | copy-start | bytes 49156
  0.7 8.4 %copy-start.3 = (f32[1,16,256]{2,1,0:T(8,128)S(1)}, f32[1,16,256]{2,1,0:T(8,128)}, u32[]{:S(2)}) copy-start(f32[1,16,256]{2,1,0:T(8,128)} %param.6) | copy-start | bytes 49156
  0.7 8.4 %copy-start = (f32[1,100,16,256]{3,2,1,0:T(8,128)S(1)}, f32[1,100,16,256]{3,2,1,0:T(8,128)}, u32[]{:S(2)}) copy-start(f32[1,100,16,256]{3,2,1,0:T(8,128)} %param.5) | copy-start | bytes 4915204
  6.5 22.4 %collective-permute-start = (f32[2880,128]{1,0:T(8,128)}, f32[2880,128]{1,0:T(8,128)S(1)}, u32[]{:S(2)}, u32[]{:S(2)}) collective-permute-start(f32[2880,128]{1,0:T(8,128)} %get-tuple-element.35), channel_id=1, source_target_pairs={{0,8},{16,24},{32,40},{48,56},{8,0},{24,16},{40,32},{56,48},{1,9},... | collective-permute-start | bytes 4423688 | tf_op jit(solution)/shard_map/ppermute | solution.py:774
  6.6 22.3 %collective-permute-start.1 = (f32[2880,128]{1,0:T(8,128)}, f32[2880,128]{1,0:T(8,128)S(1)}, u32[]{:S(2)}, u32[]{:S(2)}) collective-permute-start(f32[2880,128]{1,0:T(8,128)} %get-tuple-element.36), channel_id=1, source_target_pairs={{8,16},{24,32},{40,48},{16,8},{32,24},{48,40},{9,17},{25,33},{41,4... | collective-permute-start | bytes 4423688 | tf_op jit(solution)/shard_map/ppermute | solution.py:775
  32.6 7.6 %collective-permute-start.2 = (f32[384,128]{1,0:T(8,128)S(1)}, f32[384,128]{1,0:T(8,128)S(1)}, u32[]{:S(2)}, u32[]{:S(2)}) collective-permute-start(f32[384,128]{1,0:T(8,128)S(1)} %get-tuple-element.43), channel_id=1, source_target_pairs={{0,1},{2,3},{4,5},{6,7},{1,0},{3,2},{5,4},{7,6},{8,9},{10,11},{12,... | collective-permute-start | bytes 589832 | tf_op jit(solution)/shard_map/ppermute | solution.py:788
  34.5 11.7 %collective-permute-start.3 = (f32[384,128]{1,0:T(8,128)S(1)}, f32[384,128]{1,0:T(8,128)S(1)}, u32[]{:S(2)}, u32[]{:S(2)}) collective-permute-start(f32[384,128]{1,0:T(8,128)S(1)} %get-tuple-element.44), channel_id=1, source_target_pairs={{1,2},{3,4},{5,6},{2,1},{4,3},{6,5},{9,10},{11,12},{13,14},{10,9},... | collective-permute-start | bytes 589832 | tf_op jit(solution)/shard_map/ppermute | solution.py:789
  61.9 5.5 %collective-permute-start.4 = (f32[72,128]{1,0:T(8,128)S(1)}, f32[72,128]{1,0:T(8,128)S(1)}, u32[]{:S(2)}, u32[]{:S(2)}) collective-permute-start(f32[72,128]{1,0:T(8,128)S(1)} %get-tuple-element.48), channel_id=1, source_target_pairs={{0,64},{64,0},{1,65},{65,1},{2,66},{66,2},{3,67},{67,3},{4,68},{68... | collective-permute-start | bytes 110600 | tf_op jit(solution)/shard_map/ppermute | solution.py:809
  88.2 5.5 %collective-permute-start.5 = (f32[72,128]{1,0:T(8,128)S(1)}, f32[72,128]{1,0:T(8,128)S(1)}, u32[]{:S(2)}, u32[]{:S(2)}) collective-permute-start(f32[72,128]{1,0:T(8,128)S(1)} %get-tuple-element.52), channel_id=1, source_target_pairs={{0,64},{64,0},{1,65},{65,1},{2,66},{66,2},{3,67},{67,3},{4,68},{68... | collective-permute-start | bytes 110600 | tf_op jit(solution)/shard_map/ppermute | solution.py:809
  111.2 5.5 %collective-permute-start.6 = (f32[72,128]{1,0:T(8,128)S(1)}, f32[72,128]{1,0:T(8,128)S(1)}, u32[]{:S(2)}, u32[]{:S(2)}) collective-permute-start(f32[72,128]{1,0:T(8,128)S(1)} %get-tuple-element.55), channel_id=1, source_target_pairs={{0,64},{64,0},{1,65},{65,1},{2,66},{66,2},{3,67},{67,3},{4,68},{68... | collective-permute-start | bytes 110600 | tf_op jit(solution)/shard_map/ppermute | solution.py:809
  133.1 5.3 %collective-permute-start.7 = (f32[16,256]{1,0:T(8,128)S(1)}, f32[16,256]{1,0:T(8,128)S(1)}, u32[]{:S(2)}, u32[]{:S(2)}) collective-permute-start(f32[16,256]{1,0:T(8,128)S(1)} %get-tuple-element.59), channel_id=1, source_target_pairs={{0,64},{64,0},{1,65},{65,1},{2,66},{66,2},{3,67},{67,3},{4,68},{68... | collective-permute-start | bytes 49160 | tf_op jit(solution)/shard_map/ppermute | solution.py:809
